TPU v7x, 128 devices: a whole 4x4x4 slice. The times are simulated.
128 devices in a mesh: gz: 4 (over z_hi, core), xy: 32 (over y, z_lo, x).
Axes of the slice: x: 4, y: 4, z: 4 (z_hi: 2, z_lo: 2; z = z_hi * 2 + z_lo), core: 2. Of those that a mesh axis runs over, the one named last changes fastest.
Arguments:
- raw_volume: float32 [12, 32, 256, 256], P(None, 'gz', 'xy'), may hold values from -256 to 256
- face_slot: int32 [32, 256, 256], P('gz', 'xy'), may hold values from -1024 to 1023
- touched: int32 [4, 32, 16], P('gz', 'xy'), may hold values from 0 to 31, as said below
- block_owner: int32 [4, 32], P('gz'), may hold values from 0 to 31, as said below
Outputs:
- edge_features: float32 [4, 32, 144, 64], P('gz', 'xy')
Inputs may be any that keep to these rules, and one draw needn't show every extreme that they name: `face_slot`: a negative value marks a voxel on no contact face. `touched`: the 16 blocks of one device have 16 different owners; in each slab one owner is named by every device of the slab. `block_owner`: each tile owns exactly 1 block of its slab.
All inputs are finite; a program needn't handle non-finite values.
Results may differ from a plain program's by a relative error of at most 0.0003.
Values sent between devices are 32-bit elements; how exact they have to be, the bound alone decides.
A program may use at most 192 MiB of HBM per device.

v0:
```python
import jax
import jax.numpy as jnp
from jax import lax
from jax.sharding import PartitionSpec as P

RADIUS = 8
EB = 64
BLK_DEV = 1


far_value = 1e30


def with_halo(array, sides, width):
    for axis, dim in sides:
        peers, length = (lax.axis_size(axis), array.shape[dim])
        up = [(i, (i + 1) % peers) for i in range(peers - 1)]
        down = [(j, i) for i, j in up]
        last = lax.slice_in_dim(array, length - width, length, axis=dim)
        first = lax.slice_in_dim(array, 0, width, axis=dim)
        before = lax.ppermute(last, axis, up)
        after = lax.ppermute(first, axis, down)
        array = jnp.concatenate([before, array, after], axis=dim)
    return array


def merged(array, axis, combine):
    everything = jax.tree.map(lambda part: lax.all_gather(part, axis), array)
    first = jax.tree.map(lambda part: part[0], everything)

    def hop(k, so_far):
        return combine(so_far, jax.tree.map(lambda part: part[k], everything))

    return lax.fori_loop(1, lax.axis_size(axis), hop, first)


def kernel_taps(radius):
    sigma = radius / 3.0
    offsets = jnp.arange(2 * radius + 1).astype(jnp.float32) - radius
    gauss = jnp.exp(-offsets * offsets / (2.0 * sigma * sigma))
    gauss = gauss / jnp.sum(gauss)
    slope = -(offsets / sigma) * gauss
    curve = (offsets * offsets / (sigma * sigma) - 1.0) * gauss
    return (gauss, slope, curve)


def filter_along(field, kernel, axis, length, radius):
    total = kernel[0] * lax.slice_in_dim(field, 0, length, axis=axis)
    for offset in range(1, 2 * radius + 1):
        total = total + kernel[offset] * lax.slice_in_dim(field, offset, offset + length, axis=axis)
    return total


def line_matrix(kernel, breadth, radius):
    row_index = jnp.arange(breadth)[:, None]
    col_index = jnp.arange(breadth)[None, :]
    distance = row_index - col_index
    picked = kernel[jnp.clip(distance + radius, 0, 2 * radius)]
    return jnp.where(jnp.abs(distance) <= radius, picked, 0.0)


def voxel_features(z_smooth, z_slope, height, breadth, radius):
    gauss, slope, curve = kernel_taps(radius)
    plain = filter_along(z_smooth, gauss, 2, height, radius)
    sloped = filter_along(z_smooth, slope, 2, height, radius)
    curved = filter_along(z_smooth, curve, 2, height, radius)
    lifted = filter_along(z_slope, gauss, 2, height, radius)
    tables = jnp.concatenate(
        [
            line_matrix(gauss, breadth, radius),
            line_matrix(slope, breadth, radius),
            line_matrix(curve, breadth, radius),
        ],
        axis=1,
    )

    def apply_x(field, columns):
        flat = field.reshape(-1, breadth)
        result = jnp.dot(flat, tables[:, : columns * breadth], precision=lax.Precision.HIGHEST)
        return result.reshape(flat.shape[0], columns, breadth)

    triple = apply_x(plain, 3)
    double = apply_x(sloped, 2)
    hess_yy = apply_x(curved, 1)[:, 0]
    grad_z = apply_x(lifted, 1)[:, 0]
    smooth, grad_x, hess_xx = (triple[:, 0], triple[:, 1], triple[:, 2])
    grad_y, hess_xy = (double[:, 0], double[:, 1])
    magnitude = jnp.sqrt(grad_z * grad_z + grad_y * grad_y + grad_x * grad_x)
    half_trace = (hess_yy + hess_xx) * 0.5
    spread = (hess_yy - hess_xx) * 0.5
    deviation = jnp.sqrt(spread * spread + hess_xy * hess_xy)
    stacked = jnp.stack([smooth, magnitude, half_trace + deviation, half_trace - deviation])
    channels = z_smooth.shape[0]
    return stacked.reshape(4 * channels, -1)


def pool_faces(feature_rows, targets, slot_count):
    feature_count = feature_rows.shape[0]
    sums = (
        jnp.zeros((feature_count, slot_count), jnp.float32)
        .at[:, targets]
        .add(feature_rows, mode="drop")
    )
    maxima = (
        jnp.full((feature_count, slot_count), -far_value, jnp.float32)
        .at[:, targets]
        .max(feature_rows, mode="drop")
    )
    minima = (
        jnp.full((feature_count, slot_count), far_value, jnp.float32)
        .at[:, targets]
        .min(feature_rows, mode="drop")
    )
    counts = (
        jnp.zeros((slot_count,), jnp.float32)
        .at[targets]
        .add(jnp.ones(targets.shape, jnp.float32), mode="drop")
    )
    return (sums, maxima, minima, counts)


def finalize(sums, maxima, minima, counts):
    present = counts[..., None, :] > 0.0
    average = sums / jnp.maximum(counts, 1.0)[..., None, :]
    largest = jnp.where(present, maxima, 0.0)
    smallest = jnp.where(present, minima, 0.0)
    stacked = jnp.concatenate([average, largest, smallest], axis=-2)
    stacked = jnp.swapaxes(stacked, -3, -2)
    return stacked.reshape(stacked.shape[:-2] + (stacked.shape[-2] * stacked.shape[-1],))


def combine_stats(left, right):
    return (
        left[0] + right[0],
        jnp.maximum(left[1], right[1]),
        jnp.minimum(left[2], right[2]),
        left[3] + right[3],
    )


def per_device(raw_volume, face_slot, touched, block_owner):
    radius = RADIUS
    channels, depth, height, breadth = raw_volume.shape
    gauss, slope, curve = kernel_taps(radius)
    padded = with_halo(raw_volume, (("gz", 1), ("xy", 2)), radius)
    z_smooth = filter_along(padded, gauss, 1, depth, radius)
    z_slope = filter_along(padded, slope, 1, depth, radius)
    feature_rows = voxel_features(z_smooth, z_slope, height, breadth, radius)
    feature_count = feature_rows.shape[0]
    my_blocks = touched.reshape(-1)
    touch_count = my_blocks.shape[0]
    owners = block_owner.reshape(-1)
    block_total = owners.shape[0]
    face_slots = face_slot.reshape(-1)
    targets = jnp.where(face_slots < 0, touch_count * EB, face_slots)
    sums, maxima, minima, counts = pool_faces(feature_rows, targets, touch_count * EB)
    sums = sums.reshape(feature_count, touch_count, EB).transpose(1, 0, 2)
    maxima = maxima.reshape(feature_count, touch_count, EB).transpose(1, 0, 2)
    minima = minima.reshape(feature_count, touch_count, EB).transpose(1, 0, 2)
    counts = counts.reshape(touch_count, EB)
    my_index = lax.axis_index("xy")
    dense_sum = jnp.zeros((block_total, feature_count, EB), jnp.float32).at[my_blocks].set(sums)
    dense_max = (
        jnp.full((block_total, feature_count, EB), -far_value, jnp.float32)
        .at[my_blocks]
        .set(maxima)
    )
    dense_min = (
        jnp.full((block_total, feature_count, EB), far_value, jnp.float32).at[my_blocks].set(minima)
    )
    dense_count = jnp.zeros((block_total, EB), jnp.float32).at[my_blocks].set(counts)
    totals = merged((dense_sum, dense_max, dense_min, dense_count), "xy", combine_stats)
    owned_ids = jnp.nonzero(owners == my_index, size=BLK_DEV)[0]
    picked = (
        totals[0][owned_ids],
        totals[1][owned_ids],
        totals[2][owned_ids],
        totals[3][owned_ids],
    )
    result = finalize(picked[0], picked[1], picked[2], picked[3])
    return result[None, None]


def solution(mesh):
    placed = (P(None, "gz", "xy", None), P("gz", "xy", None), P("gz", "xy", None), P("gz", None))
    return jax.shard_map(
        per_device, mesh=mesh, in_specs=placed, out_specs=P("gz", "xy", None, None), check_vma=False
    )
```

profile of v0, /device:TPU:1, one launch (start us, length us, event | category | flops | bytes accessed | tf_op | source)
XLA Modules:
  0.0 1255.1 jit_solution(10221418742280272992)
XLA Ops:
  6.5 7.0 collective-permute-start
  13.6 1.9 collective-permute-start.1
  18.9 10.8 fusion.40
  30.4 10.8 fusion.50
  41.2 10.8 fusion.60
  54.0 3.3 collective-permute-start.2
  58.7 45.7 %collective-permute-done.2 = f32[12,24,8,256]{3,2,1,0:T(8,128)S(1)} collective-permute-done((f32[12,24,8,256]{3,2,1,0:T(8,128)S(1)}, f32[12,24,8,256]{3,2,1,0:T(8,128)S(1)}, u32[]{:S(2)}, u32[]{:S(2)}) %collective-permute-start.2) | collective-permute-done | bytes 2359328 | tf_op jit(solution)/shard_map/ppermute | solution.py:21
  104.4 4.2 collective-permute-done.3
  109.2 14.8 %multiply_add_fusion.1 = f32[12,8,24,256]{3,2,1,0:T(8,128)S(1)} fusion(f32[12,24,24,256]{3,2,1,0:T(8,128)S(1)} %pad_maximum_fusion, f32[]{:T(128)} %bitcast.23, f32[]{:T(128)} %bitcast.22, f32[]{:T(128)} %bitcast.21, f32[]{:T(128)} %bitcast.20, f32[]{:T(128)} %bitcast.19, f32[]{:T(128)} %bitcast.18, f32[]{:T(128)} %bitcast.17, f32[]{:T(128)} %bitcast.16, ...), kind=kLoop, calls=%fused_computation.22 | loop fusion | flops 19464192 | bytes 42467396 | tf_op jit(solution)/shard_map/add | solution.py:50
  124.0 12.1 multiply_add_fusion.4
  136.1 12.2 multiply_add_fusion.3
  148.2 14.8 %multiply_add_fusion = f32[12,8,24,256]{3,2,1,0:T(8,128)S(1)} fusion(f32[12,24,24,256]{3,2,1,0:T(8,128)S(1)} %pad_maximum_fusion, f32[]{:T(128)} %bitcast.37, f32[]{:T(128)} %bitcast.38, f32[]{:T(128)} %bitcast.39, f32[]{:T(128)} %bitcast.40, f32[]{:T(128)} %bitcast.41, f32[]{:T(128)} %bitcast.42, f32[]{:T(128)} %bitcast.43, f32[]{:T(128)} %bitcast.44, ...), kind=kLoop, calls=%fused_computation.21 | loop fusion | flops 19464192 | bytes 42467396 | tf_op jit(solution)/shard_map/add | solution.py:50
  163.1 12.2 multiply_add_fusion.2
  175.3 12.3 fusion.15
  187.6 2.1 fusion.148
  191.2 11.7 fusion.9
  202.9 11.8 add_bitcast_fusion
  215.0 2.4 reshape.487
  217.3 6.5 copy.21
  223.9 79.8 %scatter_custom_fusion.2 = f32[48,1024]{0,1:T(8,128)S(1)} fusion(s32[16384]{0:T(1024)S(1)} %bitcast.363, f32[48,16384]{0,1:T(8,128)} %copy.21, f32[]{:T(128)} %constant.128.clone.1), kind=kCustom, calls=%fused_computation.15 | custom fusion | flops 786432 | bytes 3342340 | tf_op jit(solution)/shard_map/scatter-max | solution.py:107
  306.2 79.8 %scatter_custom_fusion.4 = f32[48,1024]{0,1:T(8,128)S(1)} fusion(s32[16384]{0:T(1024)S(1)} %bitcast.364, f32[48,16384]{0,1:T(8,128)} %copy.21, f32[]{:T(128)} %constant.129.clone.1), kind=kCustom, calls=%fused_computation.13 | custom fusion | flops 786432 | bytes 3342340 | tf_op jit(solution)/shard_map/scatter-min | solution.py:112
  388.7 79.8 %scatter_custom_fusion = f32[48,1024]{0,1:T(8,128)S(1)} fusion(s32[16384]{0:T(1024)S(1)} %bitcast.365, f32[48,16384]{0,1:T(8,128)} %copy.21, f32[]{:T(128)} %constant.116.clone.1), kind=kCustom, calls=%fused_computation.17 | custom fusion | flops 786432 | bytes 3342340 | tf_op jit(solution)/shard_map/scatter-add | solution.py:102
  471.2 1.9 scatter_fusion.3
  476.6 87.9 %scatter_custom_fusion.6 = f32[1024]{0:T(1024)S(1)} fusion(s32[16384]{0:T(1024)S(1)} %bitcast.366, f32[16384]{0:T(1024)S(1)} %broadcast.440, f32[]{:T(128)} %constant.116.clone.1), kind=kCustom, calls=%fused_computation.160 | custom fusion | flops 16384 | bytes 4100 | tf_op jit(solution)/shard_map/scatter-add | solution.py:117
  565.2 76.9 %all-gather.3 = f32[1024,64]{1,0:T(8,128)S(1)} all-gather(f32[32,64]{1,0:T(8,128)S(1)} %scatter_custom_fusion.7), channel_id=5, replica_groups=mesh['gz'=4,'xy'=32] {'xy'}, dimensions={0}, use_global_device_ids=true | all-gather | bytes 270336 | tf_op jit(solution)/shard_map/all_gather | solution.py:28
  643.3 225.8 %all-gather.12.cloned.1.call-done = f32[1024,48,64]{2,1,0:T(8,128)} async-done(((f32[32,48,64]{2,1,0:T(8,128)}), f32[1024,48,64]{2,1,0:T(8,128)}) %all-gather.12.cloned.1.call-update) | async-done | bytes 12582928 | tf_op jit(solution)/shard_map/all_gather | solution.py:28
  870.3 274.4 %all-gather.8.cloned.1.call-done = f32[1024,48,64]{2,1,0:T(8,128)} async-done(((f32[32,48,64]{2,1,0:T(8,128)}), f32[1024,48,64]{2,1,0:T(8,128)}) %all-gather.8.cloned.1.call-update) | async-done | bytes 12582928 | tf_op jit(solution)/shard_map/all_gather | solution.py:28
  1145.8 97.2 %while.25 = (s32[]{:T(128)}, f32[32,48,64]{2,1,0:T(8,128)S(1)}, f32[32,48,64]{2,1,0:T(8,128)S(1)}, f32[32,48,64]{2,1,0:T(8,128)S(1)}, f32[32,64]{1,0:T(8,128)S(1...) while((s32[]{:T(128)}, f32[32,48,64]{2,1,0:T(8,128)S(1)}, ...), condition=%wide.region_10.11_spmd, body=%wide.region_9.10_spmd.sunk | while | flops 296965 | bytes 3563691 | solution.py:34
  1145.9 1.8 bitcast_minimum_fusion.2
  1149.0 1.8 bitcast_minimum_fusion.2
  1152.1 1.8 bitcast_minimum_fusion.2
  1155.3 1.8 bitcast_minimum_fusion.2
  (161 shorter events, 116.7 us)
Async XLA Ops:
  6.5 47.3 %copy-start.5 = (s32[1,1,16]{2,1,0:T(1,128)S(1)}, s32[1,1,16]{2,1,0:T(1,128)}, u32[]{:S(2)}) copy-start(s32[1,1,16]{2,1,0:T(1,128)} %param.8) | copy-start | bytes 196
  6.5 635.6 %all-gather.10.cloned.1.call-start = ((), (), s32[]{:S(2)}) async-start(), calls=%async_computation.1 | async-start | bytes 25952256 | tf_op jit(solution)/shard_map/all_gather | solution.py:28
  6.5 47.3 %collective-permute-start = (f32[12,8,8,256]{3,2,1,0:T(8,128)}, f32[12,8,8,256]{3,2,1,0:T(8,128)S(1)}, u32[]{:S(2)}, u32[]{:S(2)}) collective-permute-start(f32[12,8,8,256]{3,2,1,0:T(8,128)} %param.6), channel_id=1, source_target_pairs={{0,32},{32,64},{64,96},{1,33},{33,65},{65,97},{2,34},{34,66},{66,9... | collective-permute-start | bytes 2359304 | tf_op jit(solution)/shard_map/ppermute | solution.py:21
  13.6 40.4 %collective-permute-start.1 = (f32[12,8,8,256]{3,2,1,0:T(8,128)}, f32[12,8,8,256]{3,2,1,0:T(8,128)S(1)}, u32[]{:S(2)}, u32[]{:S(2)}) collective-permute-start(f32[12,8,8,256]{3,2,1,0:T(8,128)} %param.6), channel_id=1, source_target_pairs={{32,0},{64,32},{96,64},{33,1},{65,33},{97,65},{34,2},{66,34},{98,6... | collective-permute-start | bytes 2359304 | tf_op jit(solution)/shard_map/ppermute | solution.py:22
  41.2 12.7 %copy-start.4 = (f32[12,8,8,256]{3,2,1,0:T(8,128)S(1)}, f32[12,8,8,256]{3,2,1,0:T(8,128)}, u32[]{:S(2)}) copy-start(f32[12,8,8,256]{3,2,1,0:T(8,128)} %param.6) | copy-start | bytes 2359300
  54.0 50.4 %collective-permute-start.2 = (f32[12,24,8,256]{3,2,1,0:T(8,128)S(1)}, f32[12,24,8,256]{3,2,1,0:T(8,128)S(1)}, u32[]{:S(2)}, u32[]{:S(2)}) collective-permute-start(f32[12,24,8,256]{3,2,1,0:T(8,128)S(1)} %constant_dynamic-update-slice_fusion), channel_id=1, source_target_pairs={{0,1},{1,2},{2,3},{3,4},{4,5},{5,6},{6,7},{7,8},{8,9},{9,10},{10,1... | collective-permute-start | bytes 7077896 | tf_op jit(solution)/shard_map/ppermute | solution.py:21
  57.3 51.4 %collective-permute-start.3 = (f32[12,24,8,256]{3,2,1,0:T(8,128)S(1)}, f32[12,24,8,256]{3,2,1,0:T(8,128)S(1)}, u32[]{:S(2)}, u32[]{:S(2)}) collective-permute-start(f32[12,24,8,256]{3,2,1,0:T(8,128)S(1)} %constant_dynamic-update-slice_fusion), channel_id=1, source_target_pairs={{1,0},{2,1},{3,2},{4,3},{5,4},{6,5},{7,6},{8,7},{9,8},{10,9},{11,1... | collective-permute-start | bytes 7077896 | tf_op jit(solution)/shard_map/ppermute | solution.py:22
  187.6 2.2 copy-start.3
  305.2 0.9 copy-start
  306.2 562.9 %all-gather.12.cloned.1.call-start = ((), (), s32[]{:S(2)}) async-start(), calls=%async_computation.2 | async-start | bytes 25952256 | tf_op jit(solution)/shard_map/all_gather | solution.py:28
  387.7 0.9 copy-start.1
  388.7 756.0 %all-gather.8.cloned.1.call-start = ((), (), s32[]{:S(2)}) async-start(), calls=%async_computation | async-start | bytes 25952256 | tf_op jit(solution)/shard_map/all_gather | solution.py:28
  468.5 2.4 copy-start.6
  470.0 0.9 copy-start.2
Sparse Core Ops, SparseCore 0:
  306.3 283.6 all-gather.9
  591.6 277.4 all-gather.11
  870.7 273.8 all-gather.7
where the time goes:
time: 1260 us
  waiting for transfers between devices  550 us (44%)
  other arithmetic  543 us (43%)
  blocking collectives  76.9 us (6%)
  matrix products  27.1 us (2%)
  local copies, waits for them, and re-layouts  26.9 us (2%)
  between operations  16.3 us (1%)
  starting transfers between devices  13.6 us (1%)
    all_gather x3, waiting for transfers between devices, merged(): everything = jax.tree.map(lambda part: lax.all_gather(part, axis), array)  500 us
    scatter-add x1, other arithmetic, pool_faces(): counts = jnp.zeros((slot_count,), jnp.float32).at[targets].add(jnp.ones(t...  87.9 us
    scatter-add x1, other arithmetic, pool_faces(): sums = jnp.zeros((feature_count, slot_count), jnp.float32).at[:, targets]...  79.8 us
    another operation x1, other arithmetic, pool_faces(): minima = jnp.full((feature_count, slot_count), far_value, jnp.float32).at...  79.8 us
    another operation x1, other arithmetic, pool_faces(): maxima = jnp.full((feature_count, slot_count), -far_value, jnp.float32).a...  79.8 us
    add x6, other arithmetic, filter_along(): total + kernel[offset] * lax.slice_in_dim(field, offset, offset + length,...  78.4 us
    all_gather x1, blocking collectives, merged(): everything = jax.tree.map(lambda part: lax.all_gather(part, axis), array)  76.9 us
    min x31, other arithmetic, combine_stats(): jnp.minimum(left[2], right[2])  55.3 us
  transfers between devices with their start and end apart: 7, of which 4 were waited for; matrix products, arithmetic and copies ran while one was open for 24% of the time, Pallas kernels for 0%

commit v1 on v0

v1 whole, which is shorter than its diff:
```python
import functools

import jax
import jax.numpy as jnp
import ml_dtypes
import numpy as np
from jax import lax
from jax.experimental import pallas as pl
from jax.experimental.pallas import tpu as pltpu
from jax.sharding import PartitionSpec as P

RADIUS = 8
C = 12
Z = 8
Y = 8
X = 256
EB = 64
TOUCH = 16
BLOCKS = 32
TILES = 32
SLABS = 4
ZY = Z * Y
HALF = X // 2
FEATURES = 4 * C
PARTS = 4
PART = C // PARTS
ACCS = 8
ROWS = 2 * (TOUCH * EB) + 16
SENT = EB + EB // 4
FAR = -1e30
MESH = pl.DeviceIdType.MESH


def taps():
    sigma = np.float32(RADIUS / 3.0)
    offsets = np.arange(-RADIUS, RADIUS + 1).astype(np.float32)
    gauss = np.exp(-offsets * offsets / (2.0 * sigma * sigma)).astype(np.float32)
    gauss = gauss / gauss.sum()
    slope = -(offsets / sigma) * gauss
    curve = (offsets * offsets / (sigma * sigma) - 1.0) * gauss
    return [tap.astype(np.float64) for tap in (gauss, slope, curve)]


def two_terms(table):
    table = table.astype(np.float32)
    high = table.astype(ml_dtypes.bfloat16)
    low = (table - high.astype(np.float32)).astype(ml_dtypes.bfloat16)
    return high, low


def band(tap, size, start, stop):
    offset = np.arange(start, stop)[None, :] - np.arange(size)[:, None]
    return np.where(np.abs(offset) <= RADIUS, tap[np.clip(offset + RADIUS, 0, 2 * RADIUS)], 0.0)


def tables():
    gauss, slope, curve = taps()
    rows = []
    for kz, ky in ((gauss, gauss), (gauss, slope), (gauss, curve), (slope, gauss)):
        bz = band(kz, Z, -Z, 2 * Z).reshape(Z, 3, Z)
        by = band(ky, Y, -Y, 2 * Y).reshape(Y, 3, Y)
        rows.append(np.einsum("pdz,qey->pqdezy", bz, by).reshape(ZY, 9 * ZY))
    high, low = two_terms(np.concatenate(rows, axis=0))
    across = np.concatenate([high, low], axis=0)
    along = [two_terms(band(tap, X, 0, X).T) for tap in (gauss, slope, curve)]
    return across, np.concatenate([t[0] for t in along], 1), np.concatenate([t[1] for t in along], 1)


def split(values):
    high = values.astype(jnp.bfloat16)
    return high, (values - high.astype(jnp.float32)).astype(jnp.bfloat16)


def slot(dz, dt):
    return (dz + 1) * 3 + (dt + 1)


def filter_kernel(raw, across, along_hi, along_lo, out, win, send, recv):
    g, t = lax.axis_index("gz"), lax.axis_index("xy")
    mate = g + 1 - 2 * lax.rem(g, 2)
    inner = (g == 1) | (g == 2)
    other = 3 - g
    has_left, has_right = t > 0, t < TILES - 1

    barrier = pltpu.get_barrier_semaphore()

    def greet(dg, dt):
        pl.semaphore_signal(barrier, inc=1, device_id=(dg, dt), device_id_type=MESH)

    pl.when(has_left)(lambda: greet(g, t - 1))
    pl.when(has_right)(lambda: greet(g, t + 1))
    greet(mate, t)
    pl.when(inner)(lambda: greet(other, t))
    greeted = 1 + has_left.astype(jnp.int32) + has_right.astype(jnp.int32) + inner.astype(jnp.int32)
    pl.semaphore_wait(barrier, greeted)

    def part(ref, q):
        return ref.at[pl.ds(q * PART, PART)]

    def copy(kind, q, source, target, dg, dt):
        return pltpu.make_async_remote_copy(
            src_ref=part(source, q),
            dst_ref=part(win.at[target], q),
            send_sem=send.at[kind, q],
            recv_sem=recv.at[kind, q],
            device_id=(dg, dt),
            device_id_type=MESH,
        )

    def copies(q):
        up = other - g

        def made(*args):
            return lambda: copy(*args)

        return (
            (made(0, q, raw, slot(0, -1), g, t + 1), has_right, has_left),
            (made(1, q, raw, slot(0, 1), g, t - 1), has_left, has_right),
            (made(2, q, raw, slot(g - mate, 0), mate, t), True, True),
            (made(3, q, raw, slot(g - other, 0), other, t), inner, inner),
            (made(4, q, win.at[slot(0, -1)], slot(g - mate, -1), mate, t), has_left, has_left),
            (made(5, q, win.at[slot(0, 1)], slot(g - mate, 1), mate, t), has_right, has_right),
            (made(6, q, win.at[slot(up, 0)], slot(up, -1), g, t + 1), inner & has_right, inner & has_left),
            (made(7, q, win.at[slot(up, 0)], slot(up, 1), g, t - 1), inner & has_left, inner & has_right),
        )

    def start(q, kinds):
        for made, sent, _ in [copies(q)[k] for k in kinds]:
            pl.when(sent)(lambda made=made: made().start())

    def arrived(q, kinds):
        for made, _, received in [copies(q)[k] for k in kinds]:
            pl.when(received)(lambda made=made: made().wait_recv())

    def first(q, carry):
        start(q, range(4))
        return carry

    lax.fori_loop(0, PARTS, first, 0)

    def clear(index):
        def one(c, carry):
            win[index, c] = jnp.zeros((ZY, X), jnp.float32)
            return carry

        lax.fori_loop(0, C, one, 0)

    for d in (-1, 0, 1):
        pl.when(t == 0)(lambda d=d: clear(slot(d, -1)))
        pl.when(t == TILES - 1)(lambda d=d: clear(slot(d, 1)))
        pl.when(g == 0)(lambda d=d: clear(slot(-1, d)))
        pl.when(g == SLABS - 1)(lambda d=d: clear(slot(1, d)))

    def forward(q, carry):
        arrived(q, (0, 1, 3))
        start(q, (4, 5, 6, 7))
        return carry

    lax.fori_loop(0, PARTS, forward, 0)

    def dot(a, b):
        return jnp.dot(a, b, preferred_element_type=jnp.float32)

    def channel(c, carry):
        field = jnp.concatenate([raw[c] if s == 4 else win[s, c] for s in range(9)], axis=0)
        high, low = split(field)
        both = dot(across[...], high)
        mixed = both[: 4 * ZY] + both[4 * ZY :] + dot(across[: 4 * ZY], low)
        high, low = split(mixed)

        def along(rows, k):
            columns = slice(k * X, (k + 1) * X)
            return (
                dot(high[:rows], along_hi[:, columns])
                + dot(low[:rows], along_hi[:, columns])
                + dot(high[:rows], along_lo[:, columns])
            )

        by_gauss, by_slope, by_curve = along(4 * ZY, 0), along(2 * ZY, 1), along(ZY, 2)
        smooth, grad_y, hess_yy, grad_z = (by_gauss[k * ZY : (k + 1) * ZY] for k in range(4))
        grad_x, hess_xy = by_slope[:ZY], by_slope[ZY:]
        half_trace = (hess_yy + by_curve) * 0.5
        spread = (hess_yy - by_curve) * 0.5
        deviation = jnp.sqrt(spread * spread + hess_xy * hess_xy)
        magnitude = jnp.sqrt(grad_z * grad_z + grad_y * grad_y + grad_x * grad_x)
        for k, value in enumerate((smooth, magnitude, half_trace + deviation, half_trace - deviation)):
            rows = pl.ds(pl.multiple_of((k * C + c) * ZY, ZY), ZY)
            out[0, rows, :] = value[:, :HALF]
            out[1, rows, :] = value[:, HALF:]
        return carry

    def work(q, carry):
        arrived(q, (2, 4, 5, 6, 7))
        return lax.fori_loop(q * PART, (q + 1) * PART, channel, carry)

    lax.fori_loop(0, PARTS, work, 0)

    def finish(q, carry):
        for made, sent, _ in copies(q):
            pl.when(sent)(lambda made=made: made().wait_send())
        return carry

    lax.fori_loop(0, PARTS, finish, 0)


def filtered(raw):
    across, along_hi, along_lo = tables()
    vmem = pl.BlockSpec(memory_space=pltpu.VMEM)
    return pl.pallas_call(
        filter_kernel,
        out_shape=jax.ShapeDtypeStruct((2, FEATURES * ZY, HALF), jnp.float32),
        in_specs=[vmem] * 4,
        out_specs=vmem,
        scratch_shapes=[
            pltpu.VMEM((9, C, ZY, X), jnp.float32),
            pltpu.SemaphoreType.DMA((8, PARTS)),
            pltpu.SemaphoreType.DMA((8, PARTS)),
        ],
        compiler_params=pltpu.CompilerParams(
            collective_id=0, has_side_effects=True, vmem_limit_bytes=40 * 2**20
        ),
    )(raw, jnp.asarray(across), jnp.asarray(along_hi), jnp.asarray(along_lo))


def pool_kernel(features, index, touched, owner, out, row_a, row_b, merged, *accs):
    def summed(rows):
        sub = lax.broadcasted_iota(jnp.int32, (rows, HALF), 0)
        lane = lax.broadcasted_iota(jnp.int32, (rows, HALF), 1)
        return (lax.rem(sub, 2) == 1) | (lane >= 2 * FEATURES)

    pair, tile = summed(2), summed(16)
    start = jnp.where(tile, 0.0, FAR)

    def reset(i, carry):
        for acc in accs:
            acc[pl.ds(i * 16, 16), :] = start
        return carry

    lax.fori_loop(0, ROWS // 16, reset, 0)
    ones = jnp.ones((1, HALF), jnp.float32)

    def turn(half, zy, row):
        values = features[half, pl.ds(zy, FEATURES, stride=ZY), :]
        row[...] = jnp.concatenate([values, -values, values[:31], ones], axis=0).T

    def collect(half, zy, row):
        targets = index.at[zy * 2 + half]
        for v in range(HALF):
            acc = accs[v % ACCS]
            at = pl.ds(targets[v], 2)
            value = jnp.broadcast_to(row[v : v + 1, :], (2, HALF))
            old = acc[at, :]
            acc[at, :] = jnp.where(pair, old + value, jnp.maximum(old, value))

    turn(0, 0, row_a)

    def body(zy, carry):
        turn(1, zy, row_b)
        collect(0, zy, row_a)
        turn(0, jnp.minimum(zy + 1, ZY - 1), row_a)
        collect(1, zy, row_b)
        return carry

    lax.fori_loop(0, ZY, body, 0)

    lane = lax.broadcasted_iota(jnp.int32, (EB, HALF), 1)
    empty = jnp.where(lane >= 2 * FEATURES, 0.0, FAR)

    def fill(b, carry):
        out[b, :EB, :] = empty
        out[b, EB:, :] = jnp.zeros((SENT - EB, HALF), jnp.float32)
        return carry

    lax.fori_loop(0, BLOCKS, fill, 0)
    lane = lax.broadcasted_iota(jnp.int32, (EB // 4, HALF), 1)

    def place(i, carry):
        for k in range(2 * EB // 16):
            rows = pl.ds(pl.multiple_of(i * 2 * EB + k * 16, 16), 16)
            total = accs[0][rows, :]
            for acc in accs[1:]:
                more = acc[rows, :]
                total = jnp.where(tile, total + more, jnp.maximum(total, more))
            merged[pl.ds(k * 16, 16), :] = total
        to = owner[touched[i]]
        out[to, :EB, :] = merged[pl.ds(0, EB, stride=2), :]
        sums = merged[pl.ds(1, EB, stride=2), :]
        packed = jnp.zeros((EB // 4, HALF), jnp.float32)
        for j in range(4):
            group = pltpu.roll(sums[j * 16 : (j + 1) * 16], (32 * j - 16) % HALF, 1)
            packed = jnp.where((lane >= 32 * j) & (lane < 32 * j + 32), group, packed)
        out[to, EB:, :] = packed
        return carry

    lax.fori_loop(0, TOUCH, place, 0)


def pooled(features, index, touched, owner):
    vmem, smem = pl.BlockSpec(memory_space=pltpu.VMEM), pl.BlockSpec(memory_space=pltpu.SMEM)
    return pl.pallas_call(
        pool_kernel,
        out_shape=jax.ShapeDtypeStruct((BLOCKS, SENT, HALF), jnp.float32),
        in_specs=[vmem, smem, smem, smem],
        out_specs=vmem,
        scratch_shapes=[pltpu.VMEM((HALF, HALF), jnp.float32)] * 3
        + [pltpu.VMEM((ROWS, HALF), jnp.float32)] * ACCS,
        compiler_params=pltpu.CompilerParams(vmem_limit_bytes=40 * 2**20),
    )(features, index, touched, owner)


def merge_kernel(mine, out, got, send, recv):
    g, t = lax.axis_index("gz"), lax.axis_index("xy")
    barrier = pltpu.get_barrier_semaphore()

    def peer(k):
        return lax.rem(t + k, TILES)

    def greet(k, carry):
        pl.semaphore_signal(barrier, inc=1, device_id=(g, peer(k)), device_id_type=MESH)
        return carry

    lax.fori_loop(1, TILES, greet, 0)
    pl.semaphore_wait(barrier, TILES - 1)

    def copy(k):
        return pltpu.make_async_remote_copy(
            src_ref=mine.at[peer(k)],
            dst_ref=got.at[k],
            send_sem=send.at[k],
            recv_sem=recv.at[k],
            device_id=(g, peer(k)),
            device_id_type=MESH,
        )

    def start(k, carry):
        copy(k).start()
        return carry

    lax.fori_loop(1, TILES, start, 0)
    lane = lax.broadcasted_iota(jnp.int32, (SENT, HALF), 1)
    row = lax.broadcasted_iota(jnp.int32, (SENT, HALF), 0)
    summed = (lane >= 2 * FEATURES) | (row >= EB)

    def join(k, total):
        copy(k).wait_recv()
        more = got[k]
        return jnp.where(summed, total + more, jnp.maximum(total, more))

    total = lax.fori_loop(1, TILES, join, mine[t])
    extremes = total[:EB]
    packed = total[EB:]
    rest = jnp.concatenate([pltpu.roll(packed, (HALF - 32 * j) % HALF, 1) for j in range(4)], axis=0)
    both = jnp.concatenate([extremes, rest], axis=0).T
    left, right = both[:, :EB], both[:, EB:]
    count = left[HALF - 1 :]
    present = count > 0.0
    share = 1.0 / jnp.maximum(count, 1.0)
    out[:31, :] = left[2 * FEATURES : HALF - 1] * share
    out[31:FEATURES, :] = right[15:32] * share
    out[FEATURES : 2 * FEATURES, :] = jnp.where(present, left[:FEATURES], 0.0)
    out[2 * FEATURES :, :] = jnp.where(present, -left[FEATURES : 2 * FEATURES], 0.0)

    def finish(k, carry):
        copy(k).wait_send()
        return carry

    lax.fori_loop(1, TILES, finish, 0)


def merged_stats(stats):
    vmem = pl.BlockSpec(memory_space=pltpu.VMEM)
    return pl.pallas_call(
        merge_kernel,
        out_shape=jax.ShapeDtypeStruct((3 * FEATURES, EB), jnp.float32),
        in_specs=[vmem],
        out_specs=vmem,
        scratch_shapes=[
            pltpu.VMEM((TILES, SENT, HALF), jnp.float32),
            pltpu.SemaphoreType.DMA((TILES,)),
            pltpu.SemaphoreType.DMA((TILES,)),
        ],
        compiler_params=pltpu.CompilerParams(
            collective_id=1, has_side_effects=True, vmem_limit_bytes=20 * 2**20
        ),
    )(stats)


def per_device(raw_volume, face_slot, touched, block_owner):
    raw = raw_volume.reshape(C, ZY, X)
    slots = face_slot.reshape(2 * ZY, HALF)
    index = jnp.where(slots < 0, TOUCH * EB, slots) * 2
    features = filtered(raw)
    stats = pooled(features, index, touched.reshape(-1), block_owner.reshape(-1))
    return merged_stats(stats)[None, None]


def solution(mesh):
    placed = (P(None, "gz", "xy", None), P("gz", "xy", None), P("gz", "xy", None), P("gz", None))
    return jax.shard_map(
        per_device, mesh=mesh, in_specs=placed, out_specs=P("gz", "xy", None, None), check_vma=False
    )
```

time: 1260 us -> 104 us (0.08)
  waiting for transfers between devices: 550 us -> 0 us
  other arithmetic: 543 us -> 0.01 us
  Pallas kernels: 0 us -> 98.3 us
  blocking collectives: 76.9 us -> 0 us
  matrix products: 27.1 us -> 0 us
  local copies, waits for them, and re-layouts: 26.9 us -> 5.8 us
  between operations: 16.3 us -> 0.05 us
  starting transfers between devices: 13.6 us -> 0 us
    all_gather x3 -> x0, waiting for transfers between devices: 500 us -> none  [merged(): everything = jax.tree.map(lambda part: lax.all_gather(part, axis), array)]
    scatter-add x3 -> x0, other arithmetic: 170 us -> none  [the longest x1 87.9 us: pool_faces(): counts = jnp.zeros((slot_count,), jnp.float32).at[targets].add(jnp.ones(t...]
    another operation x5 -> x0, other arithmetic: 161 us -> none  [the longest x1 79.8 us: pool_faces(): minima = jnp.full((feature_count, slot_count), far_value, jnp.float32).at...]
    add x68 -> x0, other arithmetic: 119 us -> none  [the longest x6 78.4 us: filter_along(): total + kernel[offset] * lax.slice_in_dim(field, offset, offset + length,...]
    pallas_call x0 -> x3, Pallas kernels: none -> 98.3 us  [the longest x1 53.6 us: filtered(): pl.pallas_call(filter_kernel, out_shape=jax.ShapeDtypeStruct((2, FEATURES...]
    all_gather x1 -> x0, blocking collectives: 76.9 us -> none  [merged(): everything = jax.tree.map(lambda part: lax.all_gather(part, axis), array)]
    min x31 -> x0, other arithmetic: 55.3 us -> none  [combine_stats(): jnp.minimum(left[2], right[2])]
    ppermute x4 -> x0, waiting for transfers between devices: 50 us -> none  [the longest x2 45.7 us: with_halo(): before = lax.ppermute(last, axis, up)]
  transfers between devices with their start and end apart: 7 -> 0, of which waited for: 4 -> 0; matrix products, arithmetic and copies ran while one was open for 24% -> 0% of each run, Pallas kernels for 0% -> 0%
where the time goes in v1:
time: 104 us
  Pallas kernels  98.3 us (95%)
  local copies, waits for them, and re-layouts  5.8 us (6%)
    pallas_call x1, Pallas kernels, filtered(): pl.pallas_call(filter_kernel, out_shape=jax.ShapeDtypeStruct((2, FEATURES...  53.6 us
    pallas_call x1, Pallas kernels, pooled(): pl.pallas_call(pool_kernel, out_shape=jax.ShapeDtypeStruct((BLOCKS, SENT,...  22.9 us
    pallas_call x1, Pallas kernels, merged_stats(): pl.pallas_call(merge_kernel, out_shape=jax.ShapeDtypeStruct((3 * FEATURES...  21.8 us
    unnamed x12, local copies, waits for them, and re-layouts  4.21 us

profile of v1, /device:TPU:1, one launch (start us, length us, event | category | flops | bytes accessed | tf_op | source)
XLA Modules:
  0.0 104.2 jit_solution(9731039790875006315)
XLA Ops:
  0.0 0.0 copy-start.5
  0.0 0.0 copy-start.4
  0.0 0.9 reshape.13
  0.9 0.0 copy-start
  0.9 1.1 %copy-done = f32[12,8,8,256]{3,2,1,0:T(8,128)S(1)} copy-done((f32[12,8,8,256]{3,2,1,0:T(8,128)S(1)}, f32[12,8,8,256]{3,2,1,0:T(8,128)}, u32[]{:S(2)}) %copy-start) | copy-done | bytes 786456
  2.0 0.0 copy-start.1
  2.0 1.1 %copy-done.1 = bf16[512,576]{1,0:T(8,128)(2,1)S(1)} copy-done((bf16[512,576]{1,0:T(8,128)(2,1)S(1)}, bf16[512,576]{1,0:T(8,128)(2,1)}, u32[]{:S(2)}) %copy-start.1) | copy-done | bytes 589848
  3.1 0.0 copy-start.2
  3.1 1.0 copy-done.2
  4.1 0.0 copy-start.3
  4.1 1.0 copy-done.3
  5.1 53.6 %shard_map.73.features = f32[2,3072,128]{2,1,0:T(8,128)S(1)} custom-call(f32[12,64,256]{2,1,0:T(8,128)S(1)} %bitcast.4, bf16[512,576]{1,0:T(8,128)(2,1)S(1)} %copy-done.1, bf16[256,768]{1,0:T(8,128)(2,1)S(1)} %copy-done.3, bf16[256,768]{1,0:T(8,128)(2,1)S(1)} %copy-done.2), custom_call_target="tpu_custom_call" | custom-call | tf_op jit(solution)/shard_map/pallas_call | solution.py:209
  58.7 0.0 copy-done.5
  58.7 0.0 copy-done.4
  58.7 22.9 %shard_map.74.mine = f32[32,80,128]{2,1,0:T(8,128)S(1)} custom-call(f32[2,3072,128]{2,1,0:T(8,128)S(1)} %shard_map.73.features, s32[128,128]{1,0:T(8,128)S(1)} %fusion.index, s32[16]{0:T(128)S(1)} %bitcast.6, s32[32]{0:T(128)S(1)} %bitcast.7), custom_call_target="tpu_custom_call" | custom-call | tf_op jit(solution)/shard_map/pallas_call | solution.py:300
  81.7 21.8 %shard_map.75 = f32[144,64]{1,0:T(8,128)S(1)} custom-call(f32[32,80,128]{2,1,0:T(8,128)S(1)} %shard_map.74.mine), custom_call_target="tpu_custom_call" | custom-call | tf_op jit(solution)/shard_map/pallas_call | solution.py:372
  103.5 0.7 copy.8
  (1 shorter events, 0.0 us)
Async XLA Ops:
  0.0 58.7 %copy-start.5 = (s32[1,32]{1,0:T(1,128)S(1)}, s32[1,32]{1,0:T(1,128)}, u32[]{:S(2)}) copy-start(s32[1,32]{1,0:T(1,128)} %param.10) | copy-start | bytes 388
  0.0 58.7 %copy-start.4 = (s32[1,1,16]{2,1,0:T(1,128)S(1)}, s32[1,1,16]{2,1,0:T(1,128)}, u32[]{:S(2)}) copy-start(s32[1,1,16]{2,1,0:T(1,128)} %param.9) | copy-start | bytes 196
  0.9 1.1 %copy-start = (f32[12,8,8,256]{3,2,1,0:T(8,128)S(1)}, f32[12,8,8,256]{3,2,1,0:T(8,128)}, u32[]{:S(2)}) copy-start(f32[12,8,8,256]{3,2,1,0:T(8,128)} %param.7) | copy-start | bytes 2359300
  2.0 1.1 %copy-start.1 = (bf16[512,576]{1,0:T(8,128)(2,1)S(1)}, bf16[512,576]{1,0:T(8,128)(2,1)}, u32[]{:S(2)}) copy-start(bf16[512,576]{1,0:T(8,128)(2,1)} %constant.12.clone.across) | copy-start | bytes 1769476
  3.1 1.0 copy-start.2
  4.1 1.0 copy-start.3

commit v2 on v1

--- a/solution.py
+++ b/solution.py
@@ -25,6 +25,7 @@
 PARTS = 4
 PART = C // PARTS
 ACCS = 8
+ROW = 4
 ROWS = 2 * (TOUCH * EB) + 16
 SENT = EB + EB // 4
 FAR = -1e30
@@ -75,24 +76,43 @@
     return (dz + 1) * 3 + (dt + 1)
 
 
-def filter_kernel(raw, across, along_hi, along_lo, out, win, send, recv):
+def filter_kernel(
+    raw, faces, across_in, along_hi_in, along_lo_in, out, index,
+    win, features, across, along_hi, along_lo, mixed_hi, mixed_lo, send, recv, local, stored,
+):
     g, t = lax.axis_index("gz"), lax.axis_index("xy")
     mate = g + 1 - 2 * lax.rem(g, 2)
     inner = (g == 1) | (g == 2)
     other = 3 - g
     has_left, has_right = t > 0, t < TILES - 1
+    first_x, last_x = lax.rem(t, ROW) == 0, lax.rem(t, ROW) == ROW - 1
+    cross_left, cross_right = inner & first_x & has_left, inner & last_x & has_right
+
+    loads = [
+        pltpu.make_async_copy(raw, win.at[slot(0, 0)], local.at[0]),
+        pltpu.make_async_copy(across_in, across, local.at[1]),
+        pltpu.make_async_copy(along_hi_in, along_hi, local.at[2]),
+        pltpu.make_async_copy(along_lo_in, along_lo, local.at[3]),
+    ]
+    for load in loads:
+        load.start()
 
     barrier = pltpu.get_barrier_semaphore()
-
-    def greet(dg, dt):
-        pl.semaphore_signal(barrier, inc=1, device_id=(dg, dt), device_id_type=MESH)
-
-    pl.when(has_left)(lambda: greet(g, t - 1))
-    pl.when(has_right)(lambda: greet(g, t + 1))
-    greet(mate, t)
-    pl.when(inner)(lambda: greet(other, t))
-    greeted = 1 + has_left.astype(jnp.int32) + has_right.astype(jnp.int32) + inner.astype(jnp.int32)
-    pl.semaphore_wait(barrier, greeted)
+    greeted = 0
+    for condition, dg, dt in (
+        (has_left, g, t - 1),
+        (has_right, g, t + 1),
+        (inner, other, t),
+        (cross_left, other, t - 1),
+        (cross_right, other, t + 1),
+    ):
+        @pl.when(condition)
+        def _():
+            pl.semaphore_signal(barrier, inc=1, device_id=(dg, dt), device_id_type=MESH)
+
+        greeted += condition.astype(jnp.int32)
+    pl.semaphore_signal(barrier, inc=1, device_id=(mate, t), device_id_type=MESH)
+    pl.semaphore_wait(barrier, greeted + 1)
 
     def part(ref, q):
         return ref.at[pl.ds(q * PART, PART)]
@@ -120,8 +140,10 @@
             (made(3, q, raw, slot(g - other, 0), other, t), inner, inner),
             (made(4, q, win.at[slot(0, -1)], slot(g - mate, -1), mate, t), has_left, has_left),
             (made(5, q, win.at[slot(0, 1)], slot(g - mate, 1), mate, t), has_right, has_right),
-            (made(6, q, win.at[slot(up, 0)], slot(up, -1), g, t + 1), inner & has_right, inner & has_left),
-            (made(7, q, win.at[slot(up, 0)], slot(up, 1), g, t - 1), inner & has_left, inner & has_right),
+            (made(6, q, win.at[slot(up, 0)], slot(up, -1), g, t + 1), inner & ~last_x, inner & ~first_x),
+            (made(7, q, win.at[slot(up, 0)], slot(up, 1), g, t - 1), inner & ~first_x, inner & ~last_x),
+            (made(8, q, raw, slot(g - other, -1), other, t + 1), cross_right, cross_left),
+            (made(9, q, raw, slot(g - other, 1), other, t - 1), cross_left, cross_right),
         )
 
     def start(q, kinds):
@@ -133,7 +155,7 @@
             pl.when(received)(lambda made=made: made().wait_recv())
 
     def first(q, carry):
-        start(q, range(4))
+        start(q, (3, 0, 1, 8, 9, 2))
         return carry
 
     lax.fori_loop(0, PARTS, first, 0)
@@ -150,10 +172,17 @@
         pl.when(t == TILES - 1)(lambda d=d: clear(slot(d, 1)))
         pl.when(g == 0)(lambda d=d: clear(slot(-1, d)))
         pl.when(g == SLABS - 1)(lambda d=d: clear(slot(1, d)))
+    for half in range(2):
+        found = faces[:, half * HALF : (half + 1) * HALF]
+        index[half] = jnp.where(found < 0, TOUCH * EB, found) * 2
+    for load in loads:
+        load.wait()
 
     def forward(q, carry):
-        arrived(q, (0, 1, 3))
-        start(q, (4, 5, 6, 7))
+        arrived(q, (0, 1))
+        start(q, (4, 5))
+        arrived(q, (3,))
+        start(q, (6, 7))
         return carry
 
     lax.fori_loop(0, PARTS, forward, 0)
@@ -161,65 +190,88 @@
     def dot(a, b):
         return jnp.dot(a, b, preferred_element_type=jnp.float32)
 
-    def channel(c, carry):
-        field = jnp.concatenate([raw[c] if s == 4 else win[s, c] for s in range(9)], axis=0)
-        high, low = split(field)
-        both = dot(across[...], high)
-        mixed = both[: 4 * ZY] + both[4 * ZY :] + dot(across[: 4 * ZY], low)
-        high, low = split(mixed)
-
-        def along(rows, k):
+    rows = PART * ZY
+
+    def store(q, half, k):
+        at = pl.ds(pl.multiple_of(k * C * ZY + q * rows, 8), rows)
+        return pltpu.make_async_copy(features.at[half, at], out.at[half, at], stored.at[q, half * 4 + k])
+
+    def work(q, carry):
+        arrived(q, (2, 4, 5, 6, 7, 8, 9))
+        for j in range(PART):
+            c = q * PART + j
+            high, low = split(jnp.concatenate([win[s, c] for s in range(9)], axis=0))
+            both = dot(across[...], high)
+            high, low = split(both[: 4 * ZY] + both[4 * ZY :] + dot(across[: 4 * ZY], low))
+            for k in range(4):
+                mixed_hi[k, j * ZY : (j + 1) * ZY, :] = high[k * ZY : (k + 1) * ZY]
+                mixed_lo[k, j * ZY : (j + 1) * ZY, :] = low[k * ZY : (k + 1) * ZY]
+        high, low = mixed_hi[...].reshape(4 * rows, X), mixed_lo[...].reshape(4 * rows, X)
+
+        def along(n, k):
             columns = slice(k * X, (k + 1) * X)
             return (
-                dot(high[:rows], along_hi[:, columns])
-                + dot(low[:rows], along_hi[:, columns])
-                + dot(high[:rows], along_lo[:, columns])
+                dot(high[:n], along_hi[:, columns])
+                + dot(low[:n], along_hi[:, columns])
+                + dot(high[:n], along_lo[:, columns])
             )
 
-        by_gauss, by_slope, by_curve = along(4 * ZY, 0), along(2 * ZY, 1), along(ZY, 2)
-        smooth, grad_y, hess_yy, grad_z = (by_gauss[k * ZY : (k + 1) * ZY] for k in range(4))
-        grad_x, hess_xy = by_slope[:ZY], by_slope[ZY:]
+        by_gauss, by_slope, by_curve = along(4 * rows, 0), along(2 * rows, 1), along(rows, 2)
+        smooth, grad_y, hess_yy, grad_z = (by_gauss[k * rows : (k + 1) * rows] for k in range(4))
+        grad_x, hess_xy = by_slope[:rows], by_slope[rows:]
         half_trace = (hess_yy + by_curve) * 0.5
         spread = (hess_yy - by_curve) * 0.5
         deviation = jnp.sqrt(spread * spread + hess_xy * hess_xy)
         magnitude = jnp.sqrt(grad_z * grad_z + grad_y * grad_y + grad_x * grad_x)
         for k, value in enumerate((smooth, magnitude, half_trace + deviation, half_trace - deviation)):
-            rows = pl.ds(pl.multiple_of((k * C + c) * ZY, ZY), ZY)
-            out[0, rows, :] = value[:, :HALF]
-            out[1, rows, :] = value[:, HALF:]
-        return carry
-
-    def work(q, carry):
-        arrived(q, (2, 4, 5, 6, 7))
-        return lax.fori_loop(q * PART, (q + 1) * PART, channel, carry)
+            at = pl.ds(pl.multiple_of(k * C * ZY + q * rows, 8), rows)
+            features[0, at, :] = value[:, :HALF]
+            features[1, at, :] = value[:, HALF:]
+            store(q, 0, k).start()
+            store(q, 1, k).start()
+        return carry
 
     lax.fori_loop(0, PARTS, work, 0)
 
     def finish(q, carry):
         for made, sent, _ in copies(q):
             pl.when(sent)(lambda made=made: made().wait_send())
+        for k in range(4):
+            store(q, 0, k).wait()
+            store(q, 1, k).wait()
         return carry
 
     lax.fori_loop(0, PARTS, finish, 0)
 
 
-def filtered(raw):
+def filtered(raw, faces):
     across, along_hi, along_lo = tables()
-    vmem = pl.BlockSpec(memory_space=pltpu.VMEM)
+    vmem, hbm = pl.BlockSpec(memory_space=pltpu.VMEM), pl.BlockSpec(memory_space=pl.ANY)
     return pl.pallas_call(
         filter_kernel,
-        out_shape=jax.ShapeDtypeStruct((2, FEATURES * ZY, HALF), jnp.float32),
-        in_specs=[vmem] * 4,
-        out_specs=vmem,
+        out_shape=(
+            jax.ShapeDtypeStruct((2, FEATURES * ZY, HALF), jnp.float32),
+            jax.ShapeDtypeStruct((2, ZY, HALF), jnp.int32),
+        ),
+        in_specs=[hbm, vmem, hbm, hbm, hbm],
+        out_specs=(hbm, vmem),
         scratch_shapes=[
             pltpu.VMEM((9, C, ZY, X), jnp.float32),
-            pltpu.SemaphoreType.DMA((8, PARTS)),
-            pltpu.SemaphoreType.DMA((8, PARTS)),
+            pltpu.VMEM((2, FEATURES * ZY, HALF), jnp.float32),
+            pltpu.VMEM(across.shape, jnp.bfloat16),
+            pltpu.VMEM(along_hi.shape, jnp.bfloat16),
+            pltpu.VMEM(along_lo.shape, jnp.bfloat16),
+            pltpu.VMEM((4, PART * ZY, X), jnp.bfloat16),
+            pltpu.VMEM((4, PART * ZY, X), jnp.bfloat16),
+            pltpu.SemaphoreType.DMA((10, PARTS)),
+            pltpu.SemaphoreType.DMA((10, PARTS)),
+            pltpu.SemaphoreType.DMA((4,)),
+            pltpu.SemaphoreType.DMA((PARTS, 8)),
         ],
         compiler_params=pltpu.CompilerParams(
             collective_id=0, has_side_effects=True, vmem_limit_bytes=40 * 2**20
         ),
-    )(raw, jnp.asarray(across), jnp.asarray(along_hi), jnp.asarray(along_lo))
+    )(raw, faces, jnp.asarray(across), jnp.asarray(along_hi), jnp.asarray(along_lo))
 
 
 def pool_kernel(features, index, touched, owner, out, row_a, row_b, merged, *accs):
@@ -244,7 +296,7 @@
         row[...] = jnp.concatenate([values, -values, values[:31], ones], axis=0).T
 
     def collect(half, zy, row):
-        targets = index.at[zy * 2 + half]
+        targets = index.at[half * ZY + zy]
         for v in range(HALF):
             acc = accs[v % ACCS]
             at = pl.ds(targets[v], 2)
@@ -386,11 +438,8 @@
 
 
 def per_device(raw_volume, face_slot, touched, block_owner):
-    raw = raw_volume.reshape(C, ZY, X)
-    slots = face_slot.reshape(2 * ZY, HALF)
-    index = jnp.where(slots < 0, TOUCH * EB, slots) * 2
-    features = filtered(raw)
-    stats = pooled(features, index, touched.reshape(-1), block_owner.reshape(-1))
+    features, index = filtered(raw_volume.reshape(C, ZY, X), face_slot.reshape(ZY, X))
+    stats = pooled(features, index.reshape(2 * ZY, HALF), touched.reshape(-1), block_owner.reshape(-1))
     return merged_stats(stats)[None, None]
 
 

time: 104 us -> 97.8 us (0.940)
  Pallas kernels: 98.3 us -> 90.4 us
  local copies, waits for them, and re-layouts: 5.8 us -> 7.07 us
    pallas_call x1, Pallas kernels: 53.6 us -> 47.7 us  [filtered(): pl.pallas_call(filter_kernel, out_shape=(jax.ShapeDtypeStruct((2, FEATURE...]
    unnamed x12 -> x14, local copies, waits for them, and re-layouts: 4.21 us -> 6.35 us
    pallas_call x1, Pallas kernels: 21.8 us -> 19.8 us  [merged_stats(): pl.pallas_call(merge_kernel, out_shape=jax.ShapeDtypeStruct((3 * FEATURES...]
where the time goes in v2:
time: 97.8 us; the launch traced here: 97.5 us
  Pallas kernels  90.4 us (92%)
  local copies, waits for them, and re-layouts  7.07 us (7%)
    pallas_call x1, Pallas kernels, filtered(): pl.pallas_call(filter_kernel, out_shape=(jax.ShapeDtypeStruct((2, FEATURE...  47.7 us
    pallas_call x1, Pallas kernels, pooled(): pl.pallas_call(pool_kernel, out_shape=jax.ShapeDtypeStruct((BLOCKS, SENT,...  22.9 us
    pallas_call x1, Pallas kernels, merged_stats(): pl.pallas_call(merge_kernel, out_shape=jax.ShapeDtypeStruct((3 * FEATURES...  19.8 us
    unnamed x14, local copies, waits for them, and re-layouts  6.35 us

profile of v2, /device:TPU:1, one launch (start us, length us, event | category | flops | bytes accessed | tf_op | source)
XLA Modules:
  0.0 97.5 jit_solution(13953174122591677687)
XLA Ops:
  0.0 0.0 copy-start
  0.0 1.1 %copy-done = f32[12,8,8,256]{3,2,1,0:T(8,128)S(1)} copy-done((f32[12,8,8,256]{3,2,1,0:T(8,128)S(1)}, f32[12,8,8,256]{3,2,1,0:T(8,128)}, u32[]{:S(2)}) %copy-start) | copy-done | bytes 786456
  1.1 0.0 copy-start.1
  1.1 1.1 %copy-done.1 = bf16[512,576]{1,0:T(8,128)(2,1)S(1)} copy-done((bf16[512,576]{1,0:T(8,128)(2,1)S(1)}, bf16[512,576]{1,0:T(8,128)(2,1)}, u32[]{:S(2)}) %copy-start.1) | copy-done | bytes 589848
  2.2 0.0 copy-start.2
  2.2 1.0 %copy-done.2 = bf16[256,768]{1,0:T(8,128)(2,1)S(1)} copy-done((bf16[256,768]{1,0:T(8,128)(2,1)S(1)}, bf16[256,768]{1,0:T(8,128)(2,1)}, u32[]{:S(2)}) %copy-start.2) | copy-done | bytes 393240
  3.2 0.0 copy-start.3
  3.2 1.0 %copy-done.3 = bf16[256,768]{1,0:T(8,128)(2,1)S(1)} copy-done((bf16[256,768]{1,0:T(8,128)(2,1)S(1)}, bf16[256,768]{1,0:T(8,128)(2,1)}, u32[]{:S(2)}) %copy-start.3) | copy-done | bytes 393240
  4.2 0.0 copy-start.4
  4.2 0.8 copy-done.4
  5.1 47.7 %shard_map.73 = (f32[2,3072,128]{2,1,0:T(8,128)S(1)}, s32[2,64,128]{2,1,0:T(8,128)S(1)}) custom-call(f32[12,64,256]{2,1,0:T(8,128)S(1)} %bitcast.6, s32[64,256]{1,0:T(8,128)S(1)} %bitcast.9, bf16[512,576]{1,0:T(8,128)(2,1)S(1)} %copy-done.1, bf16[256,768]{1,0:T(8,128)(2,1)S(1)} %copy-done.3, bf16[256,768]{1,0:T(8,128)(2,1)S(1)} %copy-done.2), custom_call_target="tpu_custom_call" | custom-call | tf_op jit(solution)/shard_map/pallas_call | solution.py:250
  52.7 0.0 copy-start.5
  52.8 0.6 copy-done.5
  53.4 0.0 copy-start.6
  53.4 0.7 copy-done.6
  54.1 22.9 %shard_map.74.mine = f32[32,80,128]{2,1,0:T(8,128)S(1)} custom-call(f32[2,3072,128]{2,1,0:T(8,128)S(1)} %get-tuple-element.7.features, s32[128,128]{1,0:T(8,128)S(1)} %bitcast.8, s32[16]{0:T(128)S(1)} %bitcast.10, s32[32]{0:T(128)S(1)} %bitcast.11), custom_call_target="tpu_custom_call" | custom-call | tf_op jit(solution)/shard_map/pallas_call | solution.py:352
  77.0 19.8 %shard_map.75 = f32[144,64]{1,0:T(8,128)S(1)} custom-call(f32[32,80,128]{2,1,0:T(8,128)S(1)} %shard_map.74.mine), custom_call_target="tpu_custom_call" | custom-call | tf_op jit(solution)/shard_map/pallas_call | solution.py:424
  96.8 0.7 copy.8
Async XLA Ops:
  0.0 1.1 %copy-start = (f32[12,8,8,256]{3,2,1,0:T(8,128)S(1)}, f32[12,8,8,256]{3,2,1,0:T(8,128)}, u32[]{:S(2)}) copy-start(f32[12,8,8,256]{3,2,1,0:T(8,128)} %param.7) | copy-start | bytes 2359300
  1.1 1.1 %copy-start.1 = (bf16[512,576]{1,0:T(8,128)(2,1)S(1)}, bf16[512,576]{1,0:T(8,128)(2,1)}, u32[]{:S(2)}) copy-start(bf16[512,576]{1,0:T(8,128)(2,1)} %constant.6.clone.across_in) | copy-start | bytes 1769476
  2.2 1.0 %copy-start.2 = (bf16[256,768]{1,0:T(8,128)(2,1)S(1)}, bf16[256,768]{1,0:T(8,128)(2,1)}, u32[]{:S(2)}) copy-start(bf16[256,768]{1,0:T(8,128)(2,1)} %constant.8.clone.along_lo_in) | copy-start | bytes 1179652
  3.2 1.0 %copy-start.3 = (bf16[256,768]{1,0:T(8,128)(2,1)S(1)}, bf16[256,768]{1,0:T(8,128)(2,1)}, u32[]{:S(2)}) copy-start(bf16[256,768]{1,0:T(8,128)(2,1)} %constant.7.clone.along_hi_in) | copy-start | bytes 1179652
  4.2 0.8 copy-start.4
  52.7 0.7 copy-start.5
  53.4 0.7 copy-start.6

commit v3 on v2

--- a/solution.py
+++ b/solution.py
@@ -61,10 +61,15 @@
         bz = band(kz, Z, -Z, 2 * Z).reshape(Z, 3, Z)
         by = band(ky, Y, -Y, 2 * Y).reshape(Y, 3, Y)
         rows.append(np.einsum("pdz,qey->pqdezy", bz, by).reshape(ZY, 9 * ZY))
-    high, low = two_terms(np.concatenate(rows, axis=0))
-    across = np.concatenate([high, low], axis=0)
+    weights = np.concatenate(rows, axis=0).reshape(4 * ZY, 3, 3 * ZY)
+
+    def both_terms(*blocks):
+        return np.concatenate(two_terms(np.concatenate([weights[:, d + 1] for d in blocks], axis=1)), axis=0)
+
+    near = np.stack([both_terms(0, 1), both_terms(0, -1)])
+    far = np.stack([both_terms(-1), both_terms(1)])
     along = [two_terms(band(tap, X, 0, X).T) for tap in (gauss, slope, curve)]
-    return across, np.concatenate([t[0] for t in along], 1), np.concatenate([t[1] for t in along], 1)
+    return near, far, np.concatenate([t[0] for t in along], 1), np.concatenate([t[1] for t in along], 1)
 
 
 def split(values):
@@ -77,22 +82,32 @@
 
 
 def filter_kernel(
-    raw, faces, across_in, along_hi_in, along_lo_in, out, index,
-    win, features, across, along_hi, along_lo, mixed_hi, mixed_lo, send, recv, local, stored,
+    raw, faces_in, near_in, far_in, along_hi_in, along_lo_in, out, index,
+    win, faces, partial, features, near, far, along_hi, along_lo, mixed_hi, mixed_lo, send, recv, local, stored,
 ):
     g, t = lax.axis_index("gz"), lax.axis_index("xy")
-    mate = g + 1 - 2 * lax.rem(g, 2)
+    odd = lax.rem(g, 2)
+    mate = g + 1 - 2 * odd
     inner = (g == 1) | (g == 2)
     other = 3 - g
     has_left, has_right = t > 0, t < TILES - 1
-    first_x, last_x = lax.rem(t, ROW) == 0, lax.rem(t, ROW) == ROW - 1
+    column = lax.rem(t, ROW)
+    first_x, last_x = column == 0, column == ROW - 1
+    second_x, third_x = column == 1, column == 2
     cross_left, cross_right = inner & first_x & has_left, inner & last_x & has_right
 
     loads = [
-        pltpu.make_async_copy(raw, win.at[slot(0, 0)], local.at[0]),
-        pltpu.make_async_copy(across_in, across, local.at[1]),
-        pltpu.make_async_copy(along_hi_in, along_hi, local.at[2]),
-        pltpu.make_async_copy(along_lo_in, along_lo, local.at[3]),
+        pltpu.make_async_copy(source, target, local.at[k])
+        for k, (source, target) in enumerate(
+            (
+                (raw, win.at[slot(0, 0)]),
+                (faces_in, faces),
+                (near_in.at[odd], near),
+                (far_in.at[odd], far),
+                (along_hi_in, along_hi),
+                (along_lo_in, along_lo),
+            )
+        )
     ]
     for load in loads:
         load.start()
@@ -133,26 +148,31 @@
         def made(*args):
             return lambda: copy(*args)
 
+        middle = inner & (second_x | third_x)
+        left, right = win.at[slot(0, -1)], win.at[slot(0, 1)]
+        third = win.at[slot(up, 0)]
         return (
             (made(0, q, raw, slot(0, -1), g, t + 1), has_right, has_left),
             (made(1, q, raw, slot(0, 1), g, t - 1), has_left, has_right),
             (made(2, q, raw, slot(g - mate, 0), mate, t), True, True),
             (made(3, q, raw, slot(g - other, 0), other, t), inner, inner),
-            (made(4, q, win.at[slot(0, -1)], slot(g - mate, -1), mate, t), has_left, has_left),
-            (made(5, q, win.at[slot(0, 1)], slot(g - mate, 1), mate, t), has_right, has_right),
-            (made(6, q, win.at[slot(up, 0)], slot(up, -1), g, t + 1), inner & ~last_x, inner & ~first_x),
-            (made(7, q, win.at[slot(up, 0)], slot(up, 1), g, t - 1), inner & ~first_x, inner & ~last_x),
+            (made(4, q, left, slot(g - mate, -1), mate, t), has_left, has_left),
+            (made(5, q, right, slot(g - mate, 1), mate, t), has_right, has_right),
+            (made(6, q, third, slot(up, -1), g, t + 1), middle, inner & (third_x | last_x)),
+            (made(7, q, third, slot(up, 1), g, t - 1), middle, inner & (first_x | second_x)),
             (made(8, q, raw, slot(g - other, -1), other, t + 1), cross_right, cross_left),
             (made(9, q, raw, slot(g - other, 1), other, t - 1), cross_left, cross_right),
+            (made(10, q, left, slot(g - other, -1), other, t), inner & second_x, inner & second_x),
+            (made(11, q, right, slot(g - other, 1), other, t), inner & third_x, inner & third_x),
         )
 
     def start(q, kinds):
         for made, sent, _ in [copies(q)[k] for k in kinds]:
             pl.when(sent)(lambda made=made: made().start())
 
-    def arrived(q, kinds):
+    def arrived(q, kinds, where=True):
         for made, _, received in [copies(q)[k] for k in kinds]:
-            pl.when(received)(lambda made=made: made().wait_recv())
+            pl.when(received & where)(lambda made=made: made().wait_recv())
 
     def first(q, carry):
         start(q, (3, 0, 1, 8, 9, 2))
@@ -160,35 +180,43 @@
 
     lax.fori_loop(0, PARTS, first, 0)
 
-    def clear(index):
+    def clear(target):
         def one(c, carry):
-            win[index, c] = jnp.zeros((ZY, X), jnp.float32)
+            win[target, c] = jnp.zeros((ZY, X), jnp.float32)
             return carry
 
         lax.fori_loop(0, C, one, 0)
 
-    for d in (-1, 0, 1):
+    for d in (0, mate - g):
         pl.when(t == 0)(lambda d=d: clear(slot(d, -1)))
         pl.when(t == TILES - 1)(lambda d=d: clear(slot(d, 1)))
-        pl.when(g == 0)(lambda d=d: clear(slot(-1, d)))
-        pl.when(g == SLABS - 1)(lambda d=d: clear(slot(1, d)))
+    pl.when(inner & (t == 0))(lambda: clear(slot(other - g, -1)))
+    pl.when(inner & (t == TILES - 1))(lambda: clear(slot(other - g, 1)))
+    for load in loads:
+        load.wait()
     for half in range(2):
         found = faces[:, half * HALF : (half + 1) * HALF]
         index[half] = jnp.where(found < 0, TOUCH * EB, found) * 2
-    for load in loads:
-        load.wait()
-
-    def forward(q, carry):
-        arrived(q, (0, 1))
-        start(q, (4, 5))
-        arrived(q, (3,))
-        start(q, (6, 7))
-        return carry
-
-    lax.fori_loop(0, PARTS, forward, 0)
 
     def dot(a, b):
         return jnp.dot(a, b, preferred_element_type=jnp.float32)
+
+    def across(weights, blocks, c):
+        high, low = split(jnp.concatenate([win[block, c] for block in blocks], axis=0))
+        both = dot(weights[...], high)
+        return both[: 4 * ZY] + both[4 * ZY :] + dot(weights[: 4 * ZY], low)
+
+    def forward(q):
+        arrived(q, (0, 1))
+        start(q, (4, 5, 10, 11))
+        arrived(q, (3,), second_x | third_x)
+        start(q, (6, 7))
+
+    def begin(q):
+        arrived(q, (2, 4, 5))
+        for j in range(PART):
+            c = q * PART + j
+            partial[c] = across(near, [slot(d, dt) for d in (0, mate - g) for dt in (-1, 0, 1)], c)
 
     rows = PART * ZY
 
@@ -197,12 +225,17 @@
         return pltpu.make_async_copy(features.at[half, at], out.at[half, at], stored.at[q, half * 4 + k])
 
     def work(q, carry):
-        arrived(q, (2, 4, 5, 6, 7, 8, 9))
+        arrived(q, (3,), first_x | last_x)
+        arrived(q, (6, 7, 8, 9, 10, 11))
+
+        @pl.when(inner)
+        def _():
+            for j in range(PART):
+                c = q * PART + j
+                partial[c] += across(far, [slot(other - g, dt) for dt in (-1, 0, 1)], c)
+
         for j in range(PART):
-            c = q * PART + j
-            high, low = split(jnp.concatenate([win[s, c] for s in range(9)], axis=0))
-            both = dot(across[...], high)
-            high, low = split(both[: 4 * ZY] + both[4 * ZY :] + dot(across[: 4 * ZY], low))
+            high, low = split(partial[q * PART + j])
             for k in range(4):
                 mixed_hi[k, j * ZY : (j + 1) * ZY, :] = high[k * ZY : (k + 1) * ZY]
                 mixed_lo[k, j * ZY : (j + 1) * ZY, :] = low[k * ZY : (k + 1) * ZY]
@@ -231,6 +264,15 @@
             store(q, 1, k).start()
         return carry
 
+    forward(0)
+
+    def near_work(q, carry):
+        forward(q)
+        begin(q - 1)
+        return carry
+
+    lax.fori_loop(1, PARTS, near_work, 0)
+    begin(PARTS - 1)
     lax.fori_loop(0, PARTS, work, 0)
 
     def finish(q, carry):
@@ -245,33 +287,36 @@
 
 
 def filtered(raw, faces):
-    across, along_hi, along_lo = tables()
-    vmem, hbm = pl.BlockSpec(memory_space=pltpu.VMEM), pl.BlockSpec(memory_space=pl.ANY)
+    near, far, along_hi, along_lo = tables()
+    hbm = pl.BlockSpec(memory_space=pltpu.HBM)
     return pl.pallas_call(
         filter_kernel,
         out_shape=(
             jax.ShapeDtypeStruct((2, FEATURES * ZY, HALF), jnp.float32),
             jax.ShapeDtypeStruct((2, ZY, HALF), jnp.int32),
         ),
-        in_specs=[hbm, vmem, hbm, hbm, hbm],
-        out_specs=(hbm, vmem),
+        in_specs=[hbm] * 6,
+        out_specs=(pl.BlockSpec(memory_space=pl.ANY), pl.BlockSpec(memory_space=pltpu.VMEM)),
         scratch_shapes=[
             pltpu.VMEM((9, C, ZY, X), jnp.float32),
+            pltpu.VMEM((ZY, X), jnp.int32),
+            pltpu.VMEM((C, 4 * ZY, X), jnp.float32),
             pltpu.VMEM((2, FEATURES * ZY, HALF), jnp.float32),
-            pltpu.VMEM(across.shape, jnp.bfloat16),
+            pltpu.VMEM(near.shape[1:], jnp.bfloat16),
+            pltpu.VMEM(far.shape[1:], jnp.bfloat16),
             pltpu.VMEM(along_hi.shape, jnp.bfloat16),
             pltpu.VMEM(along_lo.shape, jnp.bfloat16),
             pltpu.VMEM((4, PART * ZY, X), jnp.bfloat16),
             pltpu.VMEM((4, PART * ZY, X), jnp.bfloat16),
-            pltpu.SemaphoreType.DMA((10, PARTS)),
-            pltpu.SemaphoreType.DMA((10, PARTS)),
-            pltpu.SemaphoreType.DMA((4,)),
+            pltpu.SemaphoreType.DMA((12, PARTS)),
+            pltpu.SemaphoreType.DMA((12, PARTS)),
+            pltpu.SemaphoreType.DMA((6,)),
             pltpu.SemaphoreType.DMA((PARTS, 8)),
         ],
         compiler_params=pltpu.CompilerParams(
             collective_id=0, has_side_effects=True, vmem_limit_bytes=40 * 2**20
         ),
-    )(raw, faces, jnp.asarray(across), jnp.asarray(along_hi), jnp.asarray(along_lo))
+    )(raw, faces, *(jnp.asarray(table) for table in (near, far, along_hi, along_lo)))
 
 
 def pool_kernel(features, index, touched, owner, out, row_a, row_b, merged, *accs):
@@ -399,18 +444,16 @@
         return jnp.where(summed, total + more, jnp.maximum(total, more))
 
     total = lax.fori_loop(1, TILES, join, mine[t])
-    extremes = total[:EB]
-    packed = total[EB:]
-    rest = jnp.concatenate([pltpu.roll(packed, (HALF - 32 * j) % HALF, 1) for j in range(4)], axis=0)
-    both = jnp.concatenate([extremes, rest], axis=0).T
-    left, right = both[:, :EB], both[:, EB:]
-    count = left[HALF - 1 :]
+    extremes, packed = total[:EB], total[EB:]
+    rest = jnp.concatenate([pltpu.roll(packed, (HALF + 16 - 32 * j) % HALF, 1) for j in range(4)], axis=0)
+    count = extremes[:, HALF - 1 :]
     present = count > 0.0
-    share = 1.0 / jnp.maximum(count, 1.0)
-    out[:31, :] = left[2 * FEATURES : HALF - 1] * share
-    out[31:FEATURES, :] = right[15:32] * share
-    out[FEATURES : 2 * FEATURES, :] = jnp.where(present, left[:FEATURES], 0.0)
-    out[2 * FEATURES :, :] = jnp.where(present, -left[FEATURES : 2 * FEATURES], 0.0)
+    lane = lax.broadcasted_iota(jnp.int32, (EB, HALF), 1)
+    means = jnp.where(lane < 31, pltpu.roll(extremes, HALF - 2 * FEATURES, 1), rest) / jnp.maximum(count, 1.0)
+    signed = jnp.where(present, jnp.where(lane < FEATURES, extremes, -extremes), 0.0)
+    shifted = pltpu.roll(signed, FEATURES, 1)
+    out[:, :HALF] = jnp.where(lane < FEATURES, means, shifted)
+    out[:, HALF:] = shifted[:, : 3 * FEATURES - HALF]
 
     def finish(k, carry):
         copy(k).wait_send()
@@ -423,7 +466,7 @@
     vmem = pl.BlockSpec(memory_space=pltpu.VMEM)
     return pl.pallas_call(
         merge_kernel,
-        out_shape=jax.ShapeDtypeStruct((3 * FEATURES, EB), jnp.float32),
+        out_shape=jax.ShapeDtypeStruct((EB, 3 * FEATURES), jnp.float32),
         in_specs=[vmem],
         out_specs=vmem,
         scratch_shapes=[
@@ -440,7 +483,7 @@
 def per_device(raw_volume, face_slot, touched, block_owner):
     features, index = filtered(raw_volume.reshape(C, ZY, X), face_slot.reshape(ZY, X))
     stats = pooled(features, index.reshape(2 * ZY, HALF), touched.reshape(-1), block_owner.reshape(-1))
-    return merged_stats(stats)[None, None]
+    return merged_stats(stats).T[None, None]
 
 
 def solution(mesh):

time: 97.8 us -> 101 us (1.033)
  Pallas kernels: 90.4 us -> 92.3 us
    pallas_call x1, Pallas kernels: 19.8 us -> 31.9 us  [merged_stats(): pl.pallas_call(merge_kernel, out_shape=jax.ShapeDtypeStruct((EB, 3 * FEAT...]
    pallas_call x1, Pallas kernels: 47.7 us -> 37.4 us  [filtered(): pl.pallas_call(filter_kernel, out_shape=(jax.ShapeDtypeStruct((2, FEATURE...]
    unnamed x14 -> x17, local copies, waits for them, and re-layouts: 6.35 us -> 8.07 us
where the time goes in v3:
time: 101 us; the launch traced here: 100 us
  Pallas kernels  92.3 us (91%)
  local copies, waits for them, and re-layouts  8.07 us (8%)
    pallas_call x1, Pallas kernels, filtered(): pl.pallas_call(filter_kernel, out_shape=(jax.ShapeDtypeStruct((2, FEATURE...  37.4 us
    pallas_call x1, Pallas kernels, merged_stats(): pl.pallas_call(merge_kernel, out_shape=jax.ShapeDtypeStruct((EB, 3 * FEAT...  31.9 us
    pallas_call x1, Pallas kernels, pooled(): pl.pallas_call(pool_kernel, out_shape=jax.ShapeDtypeStruct((BLOCKS, SENT,...  22.9 us
    unnamed x17, local copies, waits for them, and re-layouts  8.07 us

profile of v3, /device:TPU:1, one launch (start us, length us, event | category | flops | bytes accessed | tf_op | source)
XLA Modules:
  0.0 100.4 jit_solution(1253078017382745438)
XLA Ops:
  0.0 0.0 copy-start
  0.0 1.1 %copy-done = f32[12,8,8,256]{3,2,1,0:T(8,128)S(1)} copy-done((f32[12,8,8,256]{3,2,1,0:T(8,128)S(1)}, f32[12,8,8,256]{3,2,1,0:T(8,128)}, u32[]{:S(2)}) %copy-start) | copy-done | bytes 786456
  1.1 0.0 copy-start.1
  1.1 1.1 %copy-done.1 = bf16[2,512,384]{2,1,0:T(8,128)(2,1)S(1)} copy-done((bf16[2,512,384]{2,1,0:T(8,128)(2,1)S(1)}, bf16[2,512,384]{2,1,0:T(8,128)(2,1)}, u32[]{:S(2)}) %copy-start.1) | copy-done | bytes 786456
  2.3 0.0 copy-start.2
  2.3 1.0 %copy-done.2 = bf16[2,512,192]{2,1,0:T(8,128)(2,1)S(1)} copy-done((bf16[2,512,192]{2,1,0:T(8,128)(2,1)S(1)}, bf16[2,512,192]{2,1,0:T(8,128)(2,1)}, u32[]{:S(2)}) %copy-start.2) | copy-done | bytes 393240
  3.3 0.0 copy-start.3
  3.3 1.0 copy-done.3
  4.3 0.0 copy-start.4
  4.3 1.0 copy-done.4
  5.3 0.0 copy-start.5
  5.3 0.8 copy-done.5
  6.1 37.4 %shard_map.82 = (f32[2,3072,128]{2,1,0:T(8,128)S(1)}, s32[2,64,128]{2,1,0:T(8,128)S(1)}) custom-call(f32[12,64,256]{2,1,0:T(8,128)S(1)} %bitcast.8, s32[64,256]{1,0:T(8,128)S(1)} %bitcast.11, bf16[2,512,384]{2,1,0:T(8,128)(2,1)S(1)} %copy-done.1, bf16[2,512,192]{2,1,0:T(8,128)(2,1)S(1)} %copy-done.2, bf16[256,768]{1,0:T(8,128)(2,1)S(1)} %copy-done.4, ...), custom_call_target="tpu_custom_call" | custom-call | tf_op jit(solution)/shard_map/pallas_call | solution.py:292
  43.6 0.0 copy-start.6
  43.6 0.6 copy-done.6
  44.2 0.0 copy-start.7
  44.2 0.7 copy-done.7
  44.9 22.9 %shard_map.83.mine = f32[32,80,128]{2,1,0:T(8,128)S(1)} custom-call(f32[2,3072,128]{2,1,0:T(8,128)S(1)} %get-tuple-element.7.features, s32[128,128]{1,0:T(8,128)S(1)} %bitcast.10, s32[16]{0:T(128)S(1)} %bitcast.12, s32[32]{0:T(128)S(1)} %bitcast.13), custom_call_target="tpu_custom_call" | custom-call | tf_op jit(solution)/shard_map/pallas_call | solution.py:397
  67.9 31.9 %shard_map.84 = f32[64,144]{1,0:T(8,128)S(1)} custom-call(f32[32,80,128]{2,1,0:T(8,128)S(1)} %shard_map.83.mine), custom_call_target="tpu_custom_call" | custom-call | tf_op jit(solution)/shard_map/pallas_call | solution.py:467
  99.8 0.6 copy.10
Async XLA Ops:
  0.0 1.1 %copy-start = (f32[12,8,8,256]{3,2,1,0:T(8,128)S(1)}, f32[12,8,8,256]{3,2,1,0:T(8,128)}, u32[]{:S(2)}) copy-start(f32[12,8,8,256]{3,2,1,0:T(8,128)} %param.8) | copy-start | bytes 2359300
  1.1 1.1 %copy-start.1 = (bf16[2,512,384]{2,1,0:T(8,128)(2,1)S(1)}, bf16[2,512,384]{2,1,0:T(8,128)(2,1)}, u32[]{:S(2)}) copy-start(bf16[2,512,384]{2,1,0:T(8,128)(2,1)} %constant.8.clone.near_in) | copy-start | bytes 2359300
  2.3 1.0 %copy-start.2 = (bf16[2,512,192]{2,1,0:T(8,128)(2,1)S(1)}, bf16[2,512,192]{2,1,0:T(8,128)(2,1)}, u32[]{:S(2)}) copy-start(bf16[2,512,192]{2,1,0:T(8,128)(2,1)} %constant.9.clone.far_in) | copy-start | bytes 1179652
  3.3 1.0 copy-start.3
  4.3 1.0 copy-start.4
  5.3 0.8 copy-start.5
  43.6 0.7 copy-start.6
  44.2 0.7 copy-start.7

commit v4 on v3

--- a/solution.py
+++ b/solution.py
@@ -29,6 +29,9 @@
 ROWS = 2 * (TOUCH * EB) + 16
 SENT = EB + EB // 4
 FAR = -1e30
+STEP = ZY + 1
+AHEAD = 4
+VMEM_BYTES = 62 * 2**20
 MESH = pl.DeviceIdType.MESH
 
 
@@ -101,7 +104,8 @@
         for k, (source, target) in enumerate(
             (
                 (raw, win.at[slot(0, 0)]),
-                (faces_in, faces),
+                (faces_in.at[:, pl.ds(0, HALF)], faces.at[0]),
+                (faces_in.at[:, pl.ds(HALF, HALF)], faces.at[1]),
                 (near_in.at[odd], near),
                 (far_in.at[odd], far),
                 (along_hi_in, along_hi),
@@ -195,8 +199,9 @@
     for load in loads:
         load.wait()
     for half in range(2):
-        found = faces[:, half * HALF : (half + 1) * HALF]
-        index[half] = jnp.where(found < 0, TOUCH * EB, found) * 2
+        for k in range(2):
+            found = faces[half, pl.ds(k, ZY // 2, stride=2), :]
+            index[half, :, k * HALF : (k + 1) * HALF] = jnp.where(found < 0, TOUCH * EB, found) * 2
 
     def dot(a, b):
         return jnp.dot(a, b, preferred_element_type=jnp.float32)
@@ -220,20 +225,17 @@
 
     rows = PART * ZY
 
-    def store(q, half, k):
-        at = pl.ds(pl.multiple_of(k * C * ZY + q * rows, 8), rows)
-        return pltpu.make_async_copy(features.at[half, at], out.at[half, at], stored.at[q, half * 4 + k])
-
-    def work(q, carry):
+    def store(half):
+        return pltpu.make_async_copy(features.at[half], out.at[half], stored.at[half])
+
+    def add_third(q):
         arrived(q, (3,), first_x | last_x)
         arrived(q, (6, 7, 8, 9, 10, 11))
-
-        @pl.when(inner)
-        def _():
-            for j in range(PART):
-                c = q * PART + j
-                partial[c] += across(far, [slot(other - g, dt) for dt in (-1, 0, 1)], c)
-
+        for j in range(PART):
+            c = q * PART + j
+            partial[c] += across(far, [slot(other - g, dt) for dt in (-1, 0, 1)], c)
+
+    def end(q):
         for j in range(PART):
             high, low = split(partial[q * PART + j])
             for k in range(4):
@@ -257,33 +259,41 @@
         deviation = jnp.sqrt(spread * spread + hess_xy * hess_xy)
         magnitude = jnp.sqrt(grad_z * grad_z + grad_y * grad_y + grad_x * grad_x)
         for k, value in enumerate((smooth, magnitude, half_trace + deviation, half_trace - deviation)):
-            at = pl.ds(pl.multiple_of(k * C * ZY + q * rows, 8), rows)
-            features[0, at, :] = value[:, :HALF]
-            features[1, at, :] = value[:, HALF:]
-            store(q, 0, k).start()
-            store(q, 1, k).start()
-        return carry
+            for j in range(PART):
+                at = pl.ds((k * C + q * PART + j) * STEP, ZY)
+                features[0, at, :] = value[j * ZY : (j + 1) * ZY, :HALF]
+                features[1, at, :] = value[j * ZY : (j + 1) * ZY, HALF:]
 
     forward(0)
 
     def near_work(q, carry):
-        forward(q)
+        pl.when(q < PARTS)(lambda: forward(q))
         begin(q - 1)
-        return carry
-
-    lax.fori_loop(1, PARTS, near_work, 0)
-    begin(PARTS - 1)
-    lax.fori_loop(0, PARTS, work, 0)
+        pl.when(~inner)(lambda: end(q - 1))
+        return carry
+
+    lax.fori_loop(1, PARTS + 1, near_work, 0)
+
+    @pl.when(inner)
+    def _():
+        def far_work(q, carry):
+            add_third(q)
+            end(q)
+            return carry
+
+        lax.fori_loop(0, PARTS, far_work, 0)
+
+    for half in range(2):
+        store(half).start()
 
     def finish(q, carry):
         for made, sent, _ in copies(q):
             pl.when(sent)(lambda made=made: made().wait_send())
-        for k in range(4):
-            store(q, 0, k).wait()
-            store(q, 1, k).wait()
         return carry
 
     lax.fori_loop(0, PARTS, finish, 0)
+    for half in range(2):
+        store(half).wait()
 
 
 def filtered(raw, faces):
@@ -292,16 +302,16 @@
     return pl.pallas_call(
         filter_kernel,
         out_shape=(
-            jax.ShapeDtypeStruct((2, FEATURES * ZY, HALF), jnp.float32),
-            jax.ShapeDtypeStruct((2, ZY, HALF), jnp.int32),
+            jax.ShapeDtypeStruct((2, FEATURES * STEP, HALF), jnp.float32),
+            jax.ShapeDtypeStruct((2, ZY // 2, X), jnp.int32),
         ),
         in_specs=[hbm] * 6,
-        out_specs=(pl.BlockSpec(memory_space=pl.ANY), pl.BlockSpec(memory_space=pltpu.VMEM)),
+        out_specs=(hbm, pl.BlockSpec(memory_space=pltpu.VMEM)),
         scratch_shapes=[
             pltpu.VMEM((9, C, ZY, X), jnp.float32),
-            pltpu.VMEM((ZY, X), jnp.int32),
+            pltpu.VMEM((2, ZY, HALF), jnp.int32),
             pltpu.VMEM((C, 4 * ZY, X), jnp.float32),
-            pltpu.VMEM((2, FEATURES * ZY, HALF), jnp.float32),
+            pltpu.VMEM((2, FEATURES * STEP, HALF), jnp.float32),
             pltpu.VMEM(near.shape[1:], jnp.bfloat16),
             pltpu.VMEM(far.shape[1:], jnp.bfloat16),
             pltpu.VMEM(along_hi.shape, jnp.bfloat16),
@@ -310,16 +320,35 @@
             pltpu.VMEM((4, PART * ZY, X), jnp.bfloat16),
             pltpu.SemaphoreType.DMA((12, PARTS)),
             pltpu.SemaphoreType.DMA((12, PARTS)),
-            pltpu.SemaphoreType.DMA((6,)),
-            pltpu.SemaphoreType.DMA((PARTS, 8)),
+            pltpu.SemaphoreType.DMA((7,)),
+            pltpu.SemaphoreType.DMA((2,)),
         ],
         compiler_params=pltpu.CompilerParams(
-            collective_id=0, has_side_effects=True, vmem_limit_bytes=40 * 2**20
+            collective_id=0, has_side_effects=True, vmem_limit_bytes=VMEM_BYTES
         ),
     )(raw, faces, *(jnp.asarray(table) for table in (near, far, along_hi, along_lo)))
 
 
-def pool_kernel(features, index, touched, owner, out, row_a, row_b, merged, *accs):
+def pool_kernel(
+    features_in, index_in, touched_in, owner_in, out,
+    features, index, touched, owner, row_a, row_b, merged, local, ahead, *rest,
+):
+    accs, targets = rest[:ACCS], rest[ACCS:]
+    loads = [
+        pltpu.make_async_copy(source, target, local.at[k])
+        for k, (source, target) in enumerate(
+            (
+                (index_in, index),
+                (features_in.at[0], features.at[pl.ds(0, FEATURES * STEP)]),
+                (features_in.at[1], features.at[pl.ds(FEATURES * STEP, FEATURES * STEP)]),
+                (touched_in, touched),
+                (owner_in, owner),
+            )
+        )
+    ]
+    for load in loads:
+        load.start()
+
     def summed(rows):
         sub = lax.broadcasted_iota(jnp.int32, (rows, HALF), 0)
         lane = lax.broadcasted_iota(jnp.int32, (rows, HALF), 1)
@@ -333,32 +362,46 @@
             acc[pl.ds(i * 16, 16), :] = start
         return carry
 
+    def fetch(k, row):
+        return pltpu.make_async_copy(index.at[row], targets[k], ahead.at[k])
+
+    loads[0].wait()
+    for k in range(AHEAD):
+        fetch(k, k).start()
     lax.fori_loop(0, ROWS // 16, reset, 0)
     ones = jnp.ones((1, HALF), jnp.float32)
 
-    def turn(half, zy, row):
-        values = features[half, pl.ds(zy, FEATURES, stride=ZY), :]
+    def turn(n, row):
+        at = n + lax.div(n, ZY) * (FEATURES * STEP - ZY)
+        values = features[pl.ds(at, FEATURES, stride=STEP), :]
         row[...] = jnp.concatenate([values, -values, values[:31], ones], axis=0).T
 
-    def collect(half, zy, row):
-        targets = index.at[half * ZY + zy]
+    def collect(target, first, row):
         for v in range(HALF):
             acc = accs[v % ACCS]
-            at = pl.ds(targets[v], 2)
+            at = pl.ds(target[first + v], 2)
             value = jnp.broadcast_to(row[v : v + 1, :], (2, HALF))
             old = acc[at, :]
             acc[at, :] = jnp.where(pair, old + value, jnp.maximum(old, value))
 
-    turn(0, 0, row_a)
-
-    def body(zy, carry):
-        turn(1, zy, row_b)
-        collect(0, zy, row_a)
-        turn(0, jnp.minimum(zy + 1, ZY - 1), row_a)
-        collect(1, zy, row_b)
-        return carry
-
-    lax.fori_loop(0, ZY, body, 0)
+    loads[1].wait()
+    turn(0, row_a)
+
+    def body(i, carry):
+        pl.when(i == ZY // (2 * AHEAD) - 1)(lambda: loads[2].wait())
+        for k in range(AHEAD):
+            n = i * AHEAD + k
+            fetch(k, n).wait()
+            turn(2 * n + 1, row_b)
+            collect(targets[k], 0, row_a)
+            turn(jnp.minimum(2 * n + 2, 2 * ZY - 1), row_a)
+            collect(targets[k], HALF, row_b)
+            pl.when(n + AHEAD < ZY)(lambda: fetch(k, n + AHEAD).start())
+        return carry
+
+    lax.fori_loop(0, ZY // AHEAD, body, 0)
+    loads[3].wait()
+    loads[4].wait()
 
     lane = lax.broadcasted_iota(jnp.int32, (EB, HALF), 1)
     empty = jnp.where(lane >= 2 * FEATURES, 0.0, FAR)
@@ -393,15 +436,23 @@
 
 
 def pooled(features, index, touched, owner):
-    vmem, smem = pl.BlockSpec(memory_space=pltpu.VMEM), pl.BlockSpec(memory_space=pltpu.SMEM)
+    hbm = pl.BlockSpec(memory_space=pltpu.HBM)
     return pl.pallas_call(
         pool_kernel,
         out_shape=jax.ShapeDtypeStruct((BLOCKS, SENT, HALF), jnp.float32),
-        in_specs=[vmem, smem, smem, smem],
-        out_specs=vmem,
-        scratch_shapes=[pltpu.VMEM((HALF, HALF), jnp.float32)] * 3
-        + [pltpu.VMEM((ROWS, HALF), jnp.float32)] * ACCS,
-        compiler_params=pltpu.CompilerParams(vmem_limit_bytes=40 * 2**20),
+        in_specs=[hbm] * 4,
+        out_specs=pl.BlockSpec(memory_space=pltpu.VMEM),
+        scratch_shapes=[
+            pltpu.VMEM((2 * FEATURES * STEP, HALF), jnp.float32),
+            pltpu.VMEM((ZY, X), jnp.int32),
+            pltpu.SMEM((TOUCH,), jnp.int32),
+            pltpu.SMEM((BLOCKS,), jnp.int32),
+        ]
+        + [pltpu.VMEM((HALF, HALF), jnp.float32)] * 3
+        + [pltpu.SemaphoreType.DMA((5,)), pltpu.SemaphoreType.DMA((AHEAD,))]
+        + [pltpu.VMEM((ROWS, HALF), jnp.float32)] * ACCS
+        + [pltpu.SMEM((X,), jnp.int32)] * AHEAD,
+        compiler_params=pltpu.CompilerParams(vmem_limit_bytes=VMEM_BYTES),
     )(features, index, touched, owner)
 
 
@@ -475,14 +526,14 @@
             pltpu.SemaphoreType.DMA((TILES,)),
         ],
         compiler_params=pltpu.CompilerParams(
-            collective_id=1, has_side_effects=True, vmem_limit_bytes=20 * 2**20
+            collective_id=1, has_side_effects=True, vmem_limit_bytes=VMEM_BYTES
         ),
     )(stats)
 
 
 def per_device(raw_volume, face_slot, touched, block_owner):
     features, index = filtered(raw_volume.reshape(C, ZY, X), face_slot.reshape(ZY, X))
-    stats = pooled(features, index.reshape(2 * ZY, HALF), touched.reshape(-1), block_owner.reshape(-1))
+    stats = pooled(features, index.reshape(ZY, X), touched.reshape(-1), block_owner.reshape(-1))
     return merged_stats(stats).T[None, None]
 
 

time: 101 us -> 88.3 us (0.87)
  local copies, waits for them, and re-layouts: 8.07 us -> 1.47 us
  Pallas kernels: 92.3 us -> 86.6 us
    unnamed x17 -> x1, local copies, waits for them, and re-layouts: 8.07 us -> 1.47 us
    pallas_call x1, Pallas kernels: 31.9 us -> 27.1 us  [merged_stats(): pl.pallas_call(merge_kernel, out_shape=jax.ShapeDtypeStruct((EB, 3 * FEAT...]
    pallas_call x1, Pallas kernels: 22.9 us -> 21.8 us  [pooled(): pl.pallas_call(pool_kernel, out_shape=jax.ShapeDtypeStruct((BLOCKS, SENT,...]
where the time goes in v4:
time: 88.3 us; the launch traced here: 88.1 us
  Pallas kernels  86.6 us (98%)
  local copies, waits for them, and re-layouts  1.47 us (2%)
    pallas_call x1, Pallas kernels, filtered(): pl.pallas_call(filter_kernel, out_shape=(jax.ShapeDtypeStruct((2, FEATURE...  37.7 us
    pallas_call x1, Pallas kernels, merged_stats(): pl.pallas_call(merge_kernel, out_shape=jax.ShapeDtypeStruct((EB, 3 * FEAT...  27.1 us
    pallas_call x1, Pallas kernels, pooled(): pl.pallas_call(pool_kernel, out_shape=jax.ShapeDtypeStruct((BLOCKS, SENT,...  21.8 us

profile of v4, /device:TPU:1, one launch (start us, length us, event | category | flops | bytes accessed | tf_op | source)
XLA Modules:
  0.0 88.1 jit_solution(16366731734378502432)
XLA Ops:
  0.0 37.7 %shard_map.82 = (f32[2,3120,128]{2,1,0:T(8,128)}, s32[2,32,256]{2,1,0:T(8,128)}) custom-call(f32[12,64,256]{2,1,0:T(8,128)} %bitcast.8, s32[64,256]{1,0:T(8,128)} %bitcast.11, bf16[2,512,384]{2,1,0:T(8,128)(2,1)} %constant.8.clone.near_in, bf16[2,512,192]{2,1,0:T(8,128)(2,1)} %constant.9.clone.far_in, bf16[256,768]{1,0:T(8,128)(2,1)} %constant.10.clone.along_hi_in, ...), custom_call_target="tpu_custom_call" | custom-call | tf_op jit(solution)/shard_map/pallas_call | solution.py:302
  37.7 21.8 %shard_map.83.mine = f32[32,80,128]{2,1,0:T(8,128)} custom-call(f32[2,3120,128]{2,1,0:T(8,128)} %get-tuple-element.7.features_in, s32[64,256]{1,0:T(8,128)} %bitcast.10, s32[16]{0:T(128)} %bitcast.12, s32[32]{0:T(128)} %bitcast.13), custom_call_target="tpu_custom_call" | custom-call | tf_op jit(solution)/shard_map/pallas_call | solution.py:440
  59.6 27.1 %shard_map.84 = f32[64,144]{1,0:T(8,128)} custom-call(f32[32,80,128]{2,1,0:T(8,128)} %shard_map.83.mine), custom_call_target="tpu_custom_call" | custom-call | tf_op jit(solution)/shard_map/pallas_call | solution.py:518
  86.7 1.5 %copy.10 = f32[1,1,144,64]{2,3,1,0:T(8,128)} copy(f32[1,1,144,64]{2,3,1,0:T(8,128)} %bitcast.9) | data formatting | bytes 73728

commit v5 on v4

--- a/solution.py
+++ b/solution.py
@@ -22,12 +22,14 @@
 ZY = Z * Y
 HALF = X // 2
 FEATURES = 4 * C
-PARTS = 4
+PARTS = 6
 PART = C // PARTS
 ACCS = 8
 ROW = 4
 ROWS = 2 * (TOUCH * EB) + 16
 SENT = EB + EB // 4
+PIECE = SENT // 2
+GROUP = 8
 FAR = -1e30
 STEP = ZY + 1
 AHEAD = 4
@@ -330,7 +332,7 @@
 
 
 def pool_kernel(
-    features_in, index_in, touched_in, owner_in, out,
+    features_in, index_in, touched_in, owner_in, upper, lower,
     features, index, touched, owner, row_a, row_b, merged, local, ahead, *rest,
 ):
     accs, targets = rest[:ACCS], rest[ACCS:]
@@ -407,8 +409,9 @@
     empty = jnp.where(lane >= 2 * FEATURES, 0.0, FAR)
 
     def fill(b, carry):
-        out[b, :EB, :] = empty
-        out[b, EB:, :] = jnp.zeros((SENT - EB, HALF), jnp.float32)
+        upper[b] = empty[:PIECE]
+        lower[b, : EB - PIECE, :] = empty[PIECE:]
+        lower[b, EB - PIECE :, :] = jnp.zeros((SENT - EB, HALF), jnp.float32)
         return carry
 
     lax.fori_loop(0, BLOCKS, fill, 0)
@@ -423,13 +426,16 @@
                 total = jnp.where(tile, total + more, jnp.maximum(total, more))
             merged[pl.ds(k * 16, 16), :] = total
         to = owner[touched[i]]
-        out[to, :EB, :] = merged[pl.ds(0, EB, stride=2), :]
+        tile_x, tile_yz = lax.rem(to, ROW), lax.div(to, ROW)
+        extremes = merged[pl.ds(0, EB, stride=2), :]
+        upper[tile_x * GROUP + tile_yz] = extremes[:PIECE]
+        lower[to, : EB - PIECE, :] = extremes[PIECE:]
         sums = merged[pl.ds(1, EB, stride=2), :]
         packed = jnp.zeros((EB // 4, HALF), jnp.float32)
         for j in range(4):
             group = pltpu.roll(sums[j * 16 : (j + 1) * 16], (32 * j - 16) % HALF, 1)
             packed = jnp.where((lane >= 32 * j) & (lane < 32 * j + 32), group, packed)
-        out[to, EB:, :] = packed
+        lower[to, EB - PIECE :, :] = packed
         return carry
 
     lax.fori_loop(0, TOUCH, place, 0)
@@ -439,9 +445,9 @@
     hbm = pl.BlockSpec(memory_space=pltpu.HBM)
     return pl.pallas_call(
         pool_kernel,
-        out_shape=jax.ShapeDtypeStruct((BLOCKS, SENT, HALF), jnp.float32),
+        out_shape=[jax.ShapeDtypeStruct((BLOCKS, PIECE, HALF), jnp.float32)] * 2,
         in_specs=[hbm] * 4,
-        out_specs=pl.BlockSpec(memory_space=pltpu.VMEM),
+        out_specs=[pl.BlockSpec(memory_space=pltpu.VMEM)] * 2,
         scratch_shapes=[
             pltpu.VMEM((2 * FEATURES * STEP, HALF), jnp.float32),
             pltpu.VMEM((ZY, X), jnp.int32),
@@ -456,45 +462,118 @@
     )(features, index, touched, owner)
 
 
-def merge_kernel(mine, out, got, send, recv):
+def merge_kernel(
+    upper, lower, out, upper_sum, lower_sum, upper_got, lower_got, upper_last, lower_last, send, recv, local
+):
     g, t = lax.axis_index("gz"), lax.axis_index("xy")
+    x, yz = lax.rem(t, ROW), lax.div(t, ROW)
+    z, y = lax.rem(yz, 2), lax.div(yz, 2)
+    zx = lax.rem(t, GROUP)
+    loads = [
+        pltpu.make_async_copy(upper.at[pl.ds(x * GROUP, GROUP)], upper_sum, local.at[0]),
+        pltpu.make_async_copy(lower.at[pl.ds(y * GROUP, GROUP)], lower_sum, local.at[1]),
+    ]
+    for load in loads:
+        load.start()
+
+    def along_x(k):
+        return lax.rem(x + k, ROW)
+
+    def along_y(k):
+        return lax.rem(y + k, ROW)
+
+    def along_yz(k):
+        return lax.rem(yz + k, GROUP)
+
+    def along_zx(k):
+        return lax.rem(zx + k, GROUP)
+
     barrier = pltpu.get_barrier_semaphore()
 
-    def peer(k):
-        return lax.rem(t + k, TILES)
-
-    def greet(k, carry):
-        pl.semaphore_signal(barrier, inc=1, device_id=(g, peer(k)), device_id_type=MESH)
-        return carry
-
-    lax.fori_loop(1, TILES, greet, 0)
-    pl.semaphore_wait(barrier, TILES - 1)
-
-    def copy(k):
+    def greet(peer):
+        pl.semaphore_signal(barrier, inc=1, device_id=(g, peer), device_id_type=MESH)
+
+    for k in range(1, ROW):
+        greet(yz * ROW + along_x(k))
+        greet(along_y(k) * GROUP + zx)
+    for k in range(ROW):
+        greet(along_y(k) * GROUP + (1 - z) * ROW + x)
+    for k in range(1, ROW):
+        greet(y * GROUP + (1 - z) * ROW + along_x(k))
+    pl.semaphore_wait(barrier, 3 * (ROW - 1) + ROW)
+
+    def copy(source, target, at, peer):
         return pltpu.make_async_remote_copy(
-            src_ref=mine.at[peer(k)],
-            dst_ref=got.at[k],
-            send_sem=send.at[k],
-            recv_sem=recv.at[k],
-            device_id=(g, peer(k)),
+            src_ref=source,
+            dst_ref=target,
+            send_sem=send.at[at],
+            recv_sem=recv.at[at],
+            device_id=(g, peer),
             device_id_type=MESH,
         )
 
-    def start(k, carry):
-        copy(k).start()
-        return carry
-
-    lax.fori_loop(1, TILES, start, 0)
-    lane = lax.broadcasted_iota(jnp.int32, (SENT, HALF), 1)
-    row = lax.broadcasted_iota(jnp.int32, (SENT, HALF), 0)
-    summed = (lane >= 2 * FEATURES) | (row >= EB)
-
-    def join(k, total):
-        copy(k).wait_recv()
-        more = got[k]
-        return jnp.where(summed, total + more, jnp.maximum(total, more))
-
-    total = lax.fori_loop(1, TILES, join, mine[t])
+    def first_upper(k):
+        source = upper.at[pl.ds(along_x(k) * GROUP, GROUP)]
+        return copy(source, upper_got.at[k - 1], k - 1, yz * ROW + along_x(k))
+
+    def first_lower(k):
+        source = lower.at[pl.ds(along_y(k) * GROUP, GROUP)]
+        return copy(source, lower_got.at[k - 1], ROW + k - 2, along_y(k) * GROUP + zx)
+
+    def last_upper(k):
+        source = upper_sum.at[along_yz(k)]
+        return copy(source, upper_last.at[k - 1], 2 * (ROW - 1) + k - 1, along_yz(k) * ROW + x)
+
+    def last_lower(k):
+        source = lower_sum.at[along_zx(k)]
+        return copy(source, lower_last.at[k - 1], 2 * (ROW - 1) + GROUP + k - 2, y * GROUP + along_zx(k))
+
+    lane = lax.broadcasted_iota(jnp.int32, (PIECE, HALF), 1)
+    row = lax.broadcasted_iota(jnp.int32, (PIECE, HALF), 0)
+    upper_adds = lane >= 2 * FEATURES
+    lower_adds = upper_adds | (row >= EB - PIECE)
+
+    def join(adds, left, right):
+        return jnp.where(adds, left + right, jnp.maximum(left, right))
+
+    order = (2, 1, 3)
+    for k in order:
+        first_upper(k).start()
+        first_lower(k).start()
+    for load in loads:
+        load.wait()
+
+    def stage(adds, first, got, summed, last):
+        for k in order:
+            first(k).wait_recv()
+
+        def one(b, carry):
+            total = summed[b]
+            for k in range(ROW - 1):
+                total = join(adds, total, got[k, b])
+            summed[b] = total
+            return carry
+
+        lax.fori_loop(0, GROUP, one, 0)
+        for k in range(1, GROUP):
+            last(k).start()
+
+    stage(upper_adds, first_upper, upper_got, upper_sum, last_upper)
+    stage(lower_adds, first_lower, lower_got, lower_sum, last_lower)
+
+    def gather(adds, total, got, last):
+        for k in range(1, GROUP):
+            last(k).wait_recv()
+            total = join(adds, total, got[k - 1])
+        return total
+
+    total = jnp.concatenate(
+        [
+            gather(upper_adds, upper_sum[yz], upper_last, last_upper),
+            gather(lower_adds, lower_sum[zx], lower_last, last_lower),
+        ],
+        axis=0,
+    )
     extremes, packed = total[:EB], total[EB:]
     rest = jnp.concatenate([pltpu.roll(packed, (HALF + 16 - 32 * j) % HALF, 1) for j in range(4)], axis=0)
     count = extremes[:, HALF - 1 :]
@@ -506,35 +585,40 @@
     out[:, :HALF] = jnp.where(lane < FEATURES, means, shifted)
     out[:, HALF:] = shifted[:, : 3 * FEATURES - HALF]
 
-    def finish(k, carry):
-        copy(k).wait_send()
-        return carry
-
-    lax.fori_loop(1, TILES, finish, 0)
-
-
-def merged_stats(stats):
-    vmem = pl.BlockSpec(memory_space=pltpu.VMEM)
+    for k in order:
+        first_upper(k).wait_send()
+        first_lower(k).wait_send()
+    for k in range(1, GROUP):
+        last_upper(k).wait_send()
+        last_lower(k).wait_send()
+
+
+def merged_stats(upper, lower):
+    hbm = pl.BlockSpec(memory_space=pltpu.HBM)
+    copies = 2 * (ROW - 1) + 2 * (GROUP - 1)
     return pl.pallas_call(
         merge_kernel,
         out_shape=jax.ShapeDtypeStruct((EB, 3 * FEATURES), jnp.float32),
-        in_specs=[vmem],
-        out_specs=vmem,
-        scratch_shapes=[
-            pltpu.VMEM((TILES, SENT, HALF), jnp.float32),
-            pltpu.SemaphoreType.DMA((TILES,)),
-            pltpu.SemaphoreType.DMA((TILES,)),
+        in_specs=[hbm] * 2,
+        out_specs=pl.BlockSpec(memory_space=pltpu.VMEM),
+        scratch_shapes=[pltpu.VMEM((GROUP, PIECE, HALF), jnp.float32)] * 2
+        + [pltpu.VMEM((ROW - 1, GROUP, PIECE, HALF), jnp.float32)] * 2
+        + [pltpu.VMEM((GROUP - 1, PIECE, HALF), jnp.float32)] * 2
+        + [
+            pltpu.SemaphoreType.DMA((copies,)),
+            pltpu.SemaphoreType.DMA((copies,)),
+            pltpu.SemaphoreType.DMA((2,)),
         ],
         compiler_params=pltpu.CompilerParams(
             collective_id=1, has_side_effects=True, vmem_limit_bytes=VMEM_BYTES
         ),
-    )(stats)
+    )(upper, lower)
 
 
 def per_device(raw_volume, face_slot, touched, block_owner):
     features, index = filtered(raw_volume.reshape(C, ZY, X), face_slot.reshape(ZY, X))
-    stats = pooled(features, index.reshape(ZY, X), touched.reshape(-1), block_owner.reshape(-1))
-    return merged_stats(stats).T[None, None]
+    upper, lower = pooled(features, index.reshape(ZY, X), touched.reshape(-1), block_owner.reshape(-1))
+    return merged_stats(upper, lower).T[None, None]
 
 
 def solution(mesh):

time: 88.3 us -> 82.6 us (0.935)
  Pallas kernels: 86.6 us -> 81 us
    pallas_call x1, Pallas kernels: 27.1 us -> 21.4 us  [merged_stats(): pl.pallas_call(merge_kernel, out_shape=jax.ShapeDtypeStruct((EB, 3 * FEAT...]
where the time goes in v5:
time: 82.6 us; the launch traced here: 82.5 us
  Pallas kernels  81 us (98%)
  local copies, waits for them, and re-layouts  1.47 us (2%)
    pallas_call x1, Pallas kernels, filtered(): pl.pallas_call(filter_kernel, out_shape=(jax.ShapeDtypeStruct((2, FEATURE...  37.8 us
    pallas_call x1, Pallas kernels, pooled(): pl.pallas_call(pool_kernel, out_shape=[jax.ShapeDtypeStruct((BLOCKS, PIEC...  21.7 us
    pallas_call x1, Pallas kernels, merged_stats(): pl.pallas_call(merge_kernel, out_shape=jax.ShapeDtypeStruct((EB, 3 * FEAT...  21.4 us

profile of v5, /device:TPU:1, one launch (start us, length us, event | category | flops | bytes accessed | tf_op | source)
XLA Modules:
  0.0 82.5 jit_solution(16189465713548266265)
XLA Ops:
  0.0 37.8 %shard_map.82 = (f32[2,3120,128]{2,1,0:T(8,128)}, s32[2,32,256]{2,1,0:T(8,128)}) custom-call(f32[12,64,256]{2,1,0:T(8,128)} %bitcast.8, s32[64,256]{1,0:T(8,128)} %bitcast.10, bf16[2,512,384]{2,1,0:T(8,128)(2,1)} %constant.8.clone.near_in, bf16[2,512,192]{2,1,0:T(8,128)(2,1)} %constant.9.clone.far_in, bf16[256,768]{1,0:T(8,128)(2,1)} %constant.10.clone.along_hi_in, ...), custom_call_target="tpu_custom_call" | custom-call | tf_op jit(solution)/shard_map/pallas_call | solution.py:304
  37.8 21.7 %shard_map.83 = (f32[32,40,128]{2,1,0:T(8,128)}, f32[32,40,128]{2,1,0:T(8,128)}) custom-call(f32[2,3120,128]{2,1,0:T(8,128)} %get-tuple-element.9.features_in, s32[64,256]{1,0:T(8,128)} %bitcast.11, s32[16]{0:T(128)} %bitcast.12, s32[32]{0:T(128)} %bitcast.13), custom_call_target="tpu_custom_call" | custom-call | tf_op jit(solution)/shard_map/pallas_call | solution.py:446
  59.6 21.4 %shard_map.84 = f32[64,144]{1,0:T(8,128)} custom-call(f32[32,40,128]{2,1,0:T(8,128)} %get-tuple-element.11.upper, f32[32,40,128]{2,1,0:T(8,128)} %get-tuple-element.12.lower), custom_call_target="tpu_custom_call" | custom-call | tf_op jit(solution)/shard_map/pallas_call | solution.py:599
  81.0 1.5 %copy.10 = f32[1,1,144,64]{2,3,1,0:T(8,128)} copy(f32[1,1,144,64]{2,3,1,0:T(8,128)} %bitcast.9) | data formatting | bytes 73728

commit v6 on v5

--- a/solution.py
+++ b/solution.py
@@ -26,7 +26,8 @@
 PART = C // PARTS
 ACCS = 8
 ROW = 4
-ROWS = 2 * (TOUCH * EB) + 16
+SPARE = 8
+ROWS = 2 * (TOUCH * EB + SPARE)
 SENT = EB + EB // 4
 PIECE = SENT // 2
 GROUP = 8
@@ -181,7 +182,7 @@
             pl.when(received & where)(lambda made=made: made().wait_recv())
 
     def first(q, carry):
-        start(q, (3, 0, 1, 8, 9, 2))
+        start(q, (3, 8, 9, 0, 1, 2))
         return carry
 
     lax.fori_loop(0, PARTS, first, 0)
@@ -200,10 +201,12 @@
     pl.when(inner & (t == TILES - 1))(lambda: clear(slot(other - g, 1)))
     for load in loads:
         load.wait()
+    lane = lax.broadcasted_iota(jnp.int32, (ZY // 2, HALF), 1)
+    spare = TOUCH * EB + lax.rem(lax.div(lane, ACCS), SPARE)
     for half in range(2):
         for k in range(2):
             found = faces[half, pl.ds(k, ZY // 2, stride=2), :]
-            index[half, :, k * HALF : (k + 1) * HALF] = jnp.where(found < 0, TOUCH * EB, found) * 2
+            index[half, :, k * HALF : (k + 1) * HALF] = jnp.where(found < 0, spare, found) * 2
 
     def dot(a, b):
         return jnp.dot(a, b, preferred_element_type=jnp.float32)
@@ -227,8 +230,28 @@
 
     rows = PART * ZY
 
-    def store(half):
-        return pltpu.make_async_copy(features.at[half], out.at[half], stored.at[half])
+    def edge(k, q):
+        row = (k * C + q * PART) * STEP
+        return row // 8 * 8 if 0 < q < PARTS else (row + 7) // 8 * 8
+
+    def stores(q):
+        made = []
+        for k in range(4):
+            rows = pl.ds(edge(k, q), edge(k, q + 1) - edge(k, q))
+            for half in range(2):
+                made.append(
+                    pltpu.make_async_copy(
+                        features.at[half, rows], out.at[half, rows], stored.at[q, 2 * k + half]
+                    )
+                )
+        return made
+
+    def leave(q):
+        for part_done in range(PARTS):
+            @pl.when(q == part_done)
+            def _():
+                for made in stores(part_done):
+                    made.start()
 
     def add_third(q):
         arrived(q, (3,), first_x | last_x)
@@ -265,6 +288,7 @@
                 at = pl.ds((k * C + q * PART + j) * STEP, ZY)
                 features[0, at, :] = value[j * ZY : (j + 1) * ZY, :HALF]
                 features[1, at, :] = value[j * ZY : (j + 1) * ZY, HALF:]
+        leave(q)
 
     forward(0)
 
@@ -285,17 +309,15 @@
 
         lax.fori_loop(0, PARTS, far_work, 0)
 
-    for half in range(2):
-        store(half).start()
-
     def finish(q, carry):
         for made, sent, _ in copies(q):
             pl.when(sent)(lambda made=made: made().wait_send())
         return carry
 
     lax.fori_loop(0, PARTS, finish, 0)
-    for half in range(2):
-        store(half).wait()
+    for q in range(PARTS):
+        for made in stores(q):
+            made.wait()
 
 
 def filtered(raw, faces):
@@ -323,7 +345,7 @@
             pltpu.SemaphoreType.DMA((12, PARTS)),
             pltpu.SemaphoreType.DMA((12, PARTS)),
             pltpu.SemaphoreType.DMA((7,)),
-            pltpu.SemaphoreType.DMA((2,)),
+            pltpu.SemaphoreType.DMA((PARTS, 8)),
         ],
         compiler_params=pltpu.CompilerParams(
             collective_id=0, has_side_effects=True, vmem_limit_bytes=VMEM_BYTES
@@ -367,10 +389,11 @@
     def fetch(k, row):
         return pltpu.make_async_copy(index.at[row], targets[k], ahead.at[k])
 
+    lax.fori_loop(0, ROWS // 32, reset, 0)
     loads[0].wait()
     for k in range(AHEAD):
         fetch(k, k).start()
-    lax.fori_loop(0, ROWS // 16, reset, 0)
+    lax.fori_loop(ROWS // 32, ROWS // 16, reset, 0)
     ones = jnp.ones((1, HALF), jnp.float32)
 
     def turn(n, row):

time: 82.6 us -> 80.5 us (0.975)
  Pallas kernels: 81 us -> 78.9 us
    pallas_call x1, Pallas kernels: 21.7 us -> 18.5 us  [pooled(): pl.pallas_call(pool_kernel, out_shape=[jax.ShapeDtypeStruct((BLOCKS, PIEC...]
    pallas_call x1, Pallas kernels: 21.4 us -> 24.3 us  [merged_stats(): pl.pallas_call(merge_kernel, out_shape=jax.ShapeDtypeStruct((EB, 3 * FEAT...]
    pallas_call x1, Pallas kernels: 37.8 us -> 36 us  [filtered(): pl.pallas_call(filter_kernel, out_shape=(jax.ShapeDtypeStruct((2, FEATURE...]
where the time goes in v6:
time: 80.5 us; the launch traced here: 80.4 us
  Pallas kernels  78.9 us (98%)
  local copies, waits for them, and re-layouts  1.47 us (2%)
    pallas_call x1, Pallas kernels, filtered(): pl.pallas_call(filter_kernel, out_shape=(jax.ShapeDtypeStruct((2, FEATURE...  36 us
    pallas_call x1, Pallas kernels, merged_stats(): pl.pallas_call(merge_kernel, out_shape=jax.ShapeDtypeStruct((EB, 3 * FEAT...  24.3 us
    pallas_call x1, Pallas kernels, pooled(): pl.pallas_call(pool_kernel, out_shape=[jax.ShapeDtypeStruct((BLOCKS, PIEC...  18.5 us

profile of v6, /device:TPU:1, one launch (start us, length us, event | category | flops | bytes accessed | tf_op | source)
XLA Modules:
  0.0 80.4 jit_solution(2977907634918226555)
XLA Ops:
  0.0 36.0 %shard_map.82 = (f32[2,3120,128]{2,1,0:T(8,128)}, s32[2,32,256]{2,1,0:T(8,128)}) custom-call(f32[12,64,256]{2,1,0:T(8,128)} %bitcast.8, s32[64,256]{1,0:T(8,128)} %bitcast.10, bf16[2,512,384]{2,1,0:T(8,128)(2,1)} %constant.8.clone.near_in, bf16[2,512,192]{2,1,0:T(8,128)(2,1)} %constant.9.clone.far_in, bf16[256,768]{1,0:T(8,128)(2,1)} %constant.10.clone.along_hi_in, ...), custom_call_target="tpu_custom_call" | custom-call | tf_op jit(solution)/shard_map/pallas_call | solution.py:326
  36.0 18.5 %shard_map.83 = (f32[32,40,128]{2,1,0:T(8,128)}, f32[32,40,128]{2,1,0:T(8,128)}) custom-call(f32[2,3120,128]{2,1,0:T(8,128)} %get-tuple-element.9.features_in, s32[64,256]{1,0:T(8,128)} %bitcast.11, s32[16]{0:T(128)} %bitcast.12, s32[32]{0:T(128)} %bitcast.13), custom_call_target="tpu_custom_call" | custom-call | tf_op jit(solution)/shard_map/pallas_call | solution.py:469
  54.6 24.3 %shard_map.84 = f32[64,144]{1,0:T(8,128)} custom-call(f32[32,40,128]{2,1,0:T(8,128)} %get-tuple-element.11.upper, f32[32,40,128]{2,1,0:T(8,128)} %get-tuple-element.12.lower), custom_call_target="tpu_custom_call" | custom-call | tf_op jit(solution)/shard_map/pallas_call | solution.py:622
  78.9 1.5 %copy.10 = f32[1,1,144,64]{2,3,1,0:T(8,128)} copy(f32[1,1,144,64]{2,3,1,0:T(8,128)} %bitcast.9) | data formatting | bytes 73728

commit v7 on v6

--- a/solution.py
+++ b/solution.py
@@ -24,6 +24,7 @@
 FEATURES = 4 * C
 PARTS = 6
 PART = C // PARTS
+DIRECT = 4
 ACCS = 8
 ROW = 4
 SPARE = 8
@@ -156,13 +157,14 @@
             return lambda: copy(*args)
 
         middle = inner & (second_x | third_x)
+        direct = q < DIRECT
         left, right = win.at[slot(0, -1)], win.at[slot(0, 1)]
         third = win.at[slot(up, 0)]
         return (
             (made(0, q, raw, slot(0, -1), g, t + 1), has_right, has_left),
             (made(1, q, raw, slot(0, 1), g, t - 1), has_left, has_right),
             (made(2, q, raw, slot(g - mate, 0), mate, t), True, True),
-            (made(3, q, raw, slot(g - other, 0), other, t), inner, inner),
+            (made(3, q, raw, slot(g - other, 0), other, t), middle | (inner & direct), middle | (inner & direct)),
             (made(4, q, left, slot(g - mate, -1), mate, t), has_left, has_left),
             (made(5, q, right, slot(g - mate, 1), mate, t), has_right, has_right),
             (made(6, q, third, slot(up, -1), g, t + 1), middle, inner & (third_x | last_x)),
@@ -171,6 +173,8 @@
             (made(9, q, raw, slot(g - other, 1), other, t - 1), cross_left, cross_right),
             (made(10, q, left, slot(g - other, -1), other, t), inner & second_x, inner & second_x),
             (made(11, q, right, slot(g - other, 1), other, t), inner & third_x, inner & third_x),
+            (made(12, q, win.at[slot(up, -1)], slot(up, 0), g, t - 1), inner & second_x & ~direct, inner & first_x & ~direct),
+            (made(13, q, win.at[slot(up, 1)], slot(up, 0), g, t + 1), inner & third_x & ~direct, inner & last_x & ~direct),
         )
 
     def start(q, kinds):
@@ -182,7 +186,7 @@
             pl.when(received & where)(lambda made=made: made().wait_recv())
 
     def first(q, carry):
-        start(q, (3, 8, 9, 0, 1, 2))
+        start(q, (3, 0, 1, 8, 9, 2))
         return carry
 
     lax.fori_loop(0, PARTS, first, 0)
@@ -255,7 +259,8 @@
 
     def add_third(q):
         arrived(q, (3,), first_x | last_x)
-        arrived(q, (6, 7, 8, 9, 10, 11))
+        arrived(q, (6, 7, 8, 9, 12, 13))
+        arrived(q, (10, 11), q < DIRECT)
         for j in range(PART):
             c = q * PART + j
             partial[c] += across(far, [slot(other - g, dt) for dt in (-1, 0, 1)], c)
@@ -302,6 +307,13 @@
 
     @pl.when(inner)
     def _():
+        def pass_on(q, carry):
+            arrived(q, (10, 11))
+            start(q, (12, 13))
+            return carry
+
+        lax.fori_loop(DIRECT, PARTS, pass_on, 0)
+
         def far_work(q, carry):
             add_third(q)
             end(q)
@@ -342,8 +354,8 @@
             pltpu.VMEM(along_lo.shape, jnp.bfloat16),
             pltpu.VMEM((4, PART * ZY, X), jnp.bfloat16),
             pltpu.VMEM((4, PART * ZY, X), jnp.bfloat16),
-            pltpu.SemaphoreType.DMA((12, PARTS)),
-            pltpu.SemaphoreType.DMA((12, PARTS)),
+            pltpu.SemaphoreType.DMA((14, PARTS)),
+            pltpu.SemaphoreType.DMA((14, PARTS)),
             pltpu.SemaphoreType.DMA((7,)),
             pltpu.SemaphoreType.DMA((PARTS, 8)),
         ],

time: 80.5 us -> 79.4 us (0.986)
  Pallas kernels: 78.9 us -> 77.8 us
    pallas_call x1, Pallas kernels: 24.3 us -> 21.2 us  [merged_stats(): pl.pallas_call(merge_kernel, out_shape=jax.ShapeDtypeStruct((EB, 3 * FEAT...]
    pallas_call x1, Pallas kernels: 36 us -> 38.1 us  [filtered(): pl.pallas_call(filter_kernel, out_shape=(jax.ShapeDtypeStruct((2, FEATURE...]
where the time goes in v7:
time: 79.4 us; the launch traced here: 79.3 us
  Pallas kernels  77.8 us (98%)
  local copies, waits for them, and re-layouts  1.47 us (2%)
    pallas_call x1, Pallas kernels, filtered(): pl.pallas_call(filter_kernel, out_shape=(jax.ShapeDtypeStruct((2, FEATURE...  38.1 us
    pallas_call x1, Pallas kernels, merged_stats(): pl.pallas_call(merge_kernel, out_shape=jax.ShapeDtypeStruct((EB, 3 * FEAT...  21.2 us
    pallas_call x1, Pallas kernels, pooled(): pl.pallas_call(pool_kernel, out_shape=[jax.ShapeDtypeStruct((BLOCKS, PIEC...  18.5 us

profile of v7, /device:TPU:1, one launch (start us, length us, event | category | flops | bytes accessed | tf_op | source)
XLA Modules:
  0.0 79.3 jit_solution(6364766108962978748)
XLA Ops:
  0.0 38.1 %shard_map.82 = (f32[2,3120,128]{2,1,0:T(8,128)}, s32[2,32,256]{2,1,0:T(8,128)}) custom-call(f32[12,64,256]{2,1,0:T(8,128)} %bitcast.8, s32[64,256]{1,0:T(8,128)} %bitcast.10, bf16[2,512,384]{2,1,0:T(8,128)(2,1)} %constant.8.clone.near_in, bf16[2,512,192]{2,1,0:T(8,128)(2,1)} %constant.9.clone.far_in, bf16[256,768]{1,0:T(8,128)(2,1)} %constant.10.clone.along_hi_in, ...), custom_call_target="tpu_custom_call" | custom-call | tf_op jit(solution)/shard_map/pallas_call | solution.py:338
  38.1 18.5 %shard_map.83 = (f32[32,40,128]{2,1,0:T(8,128)}, f32[32,40,128]{2,1,0:T(8,128)}) custom-call(f32[2,3120,128]{2,1,0:T(8,128)} %get-tuple-element.9.features_in, s32[64,256]{1,0:T(8,128)} %bitcast.11, s32[16]{0:T(128)} %bitcast.12, s32[32]{0:T(128)} %bitcast.13), custom_call_target="tpu_custom_call" | custom-call | tf_op jit(solution)/shard_map/pallas_call | solution.py:481
  56.7 21.2 %shard_map.84 = f32[64,144]{1,0:T(8,128)} custom-call(f32[32,40,128]{2,1,0:T(8,128)} %get-tuple-element.11.upper, f32[32,40,128]{2,1,0:T(8,128)} %get-tuple-element.12.lower), custom_call_target="tpu_custom_call" | custom-call | tf_op jit(solution)/shard_map/pallas_call | solution.py:634
  77.8 1.5 %copy.10 = f32[1,1,144,64]{2,3,1,0:T(8,128)} copy(f32[1,1,144,64]{2,3,1,0:T(8,128)} %bitcast.9) | data formatting | bytes 73728

commit v8 on v7

--- a/solution.py
+++ b/solution.py
@@ -24,7 +24,8 @@
 FEATURES = 4 * C
 PARTS = 6
 PART = C // PARTS
-DIRECT = 4
+DIRECT = 3
+CROSSED = 2
 ACCS = 8
 ROW = 4
 SPARE = 8
@@ -157,7 +158,9 @@
             return lambda: copy(*args)
 
         middle = inner & (second_x | third_x)
-        direct = q < DIRECT
+        direct, crossed = q < DIRECT, q < CROSSED
+        from_left = inner & has_left & (second_x | (first_x & ~crossed))
+        from_right = inner & has_right & (third_x | (last_x & ~crossed))
         left, right = win.at[slot(0, -1)], win.at[slot(0, 1)]
         third = win.at[slot(up, 0)]
         return (
@@ -169,10 +172,10 @@
             (made(5, q, right, slot(g - mate, 1), mate, t), has_right, has_right),
             (made(6, q, third, slot(up, -1), g, t + 1), middle, inner & (third_x | last_x)),
             (made(7, q, third, slot(up, 1), g, t - 1), middle, inner & (first_x | second_x)),
-            (made(8, q, raw, slot(g - other, -1), other, t + 1), cross_right, cross_left),
-            (made(9, q, raw, slot(g - other, 1), other, t - 1), cross_left, cross_right),
-            (made(10, q, left, slot(g - other, -1), other, t), inner & second_x, inner & second_x),
-            (made(11, q, right, slot(g - other, 1), other, t), inner & third_x, inner & third_x),
+            (made(8, q, raw, slot(g - other, -1), other, t + 1), cross_right & crossed, cross_left & crossed),
+            (made(9, q, raw, slot(g - other, 1), other, t - 1), cross_left & crossed, cross_right & crossed),
+            (made(10, q, left, slot(g - other, -1), other, t), from_left, from_left),
+            (made(11, q, right, slot(g - other, 1), other, t), from_right, from_right),
             (made(12, q, win.at[slot(up, -1)], slot(up, 0), g, t - 1), inner & second_x & ~direct, inner & first_x & ~direct),
             (made(13, q, win.at[slot(up, 1)], slot(up, 0), g, t + 1), inner & third_x & ~direct, inner & last_x & ~direct),
         )
@@ -260,7 +263,7 @@
     def add_third(q):
         arrived(q, (3,), first_x | last_x)
         arrived(q, (6, 7, 8, 9, 12, 13))
-        arrived(q, (10, 11), q < DIRECT)
+        arrived(q, (10, 11), (q < DIRECT) | first_x | last_x)
         for j in range(PART):
             c = q * PART + j
             partial[c] += across(far, [slot(other - g, dt) for dt in (-1, 0, 1)], c)
@@ -308,7 +311,7 @@
     @pl.when(inner)
     def _():
         def pass_on(q, carry):
-            arrived(q, (10, 11))
+            arrived(q, (10, 11), second_x | third_x)
             start(q, (12, 13))
             return carry
 

time: 79.4 us -> 75.9 us (0.956)
  Pallas kernels: 77.8 us -> 74.3 us
    pallas_call x1, Pallas kernels: 21.2 us -> 16.2 us  [merged_stats(): pl.pallas_call(merge_kernel, out_shape=jax.ShapeDtypeStruct((EB, 3 * FEAT...]
    pallas_call x1, Pallas kernels: 38.1 us -> 39.5 us  [filtered(): pl.pallas_call(filter_kernel, out_shape=(jax.ShapeDtypeStruct((2, FEATURE...]
where the time goes in v8:
time: 75.9 us; the launch traced here: 75.8 us
  Pallas kernels  74.3 us (98%)
  local copies, waits for them, and re-layouts  1.47 us (2%)
    pallas_call x1, Pallas kernels, filtered(): pl.pallas_call(filter_kernel, out_shape=(jax.ShapeDtypeStruct((2, FEATURE...  39.5 us
    pallas_call x1, Pallas kernels, pooled(): pl.pallas_call(pool_kernel, out_shape=[jax.ShapeDtypeStruct((BLOCKS, PIEC...  18.6 us
    pallas_call x1, Pallas kernels, merged_stats(): pl.pallas_call(merge_kernel, out_shape=jax.ShapeDtypeStruct((EB, 3 * FEAT...  16.2 us

profile of v8, /device:TPU:1, one launch (start us, length us, event | category | flops | bytes accessed | tf_op | source)
XLA Modules:
  0.0 75.8 jit_solution(14632803658586205598)
XLA Ops:
  0.0 39.5 %shard_map.82 = (f32[2,3120,128]{2,1,0:T(8,128)}, s32[2,32,256]{2,1,0:T(8,128)}) custom-call(f32[12,64,256]{2,1,0:T(8,128)} %bitcast.8, s32[64,256]{1,0:T(8,128)} %bitcast.10, bf16[2,512,384]{2,1,0:T(8,128)(2,1)} %constant.8.clone.near_in, bf16[2,512,192]{2,1,0:T(8,128)(2,1)} %constant.9.clone.far_in, bf16[256,768]{1,0:T(8,128)(2,1)} %constant.10.clone.along_hi_in, ...), custom_call_target="tpu_custom_call" | custom-call | tf_op jit(solution)/shard_map/pallas_call | solution.py:341
  39.5 18.6 %shard_map.83 = (f32[32,40,128]{2,1,0:T(8,128)}, f32[32,40,128]{2,1,0:T(8,128)}) custom-call(f32[2,3120,128]{2,1,0:T(8,128)} %get-tuple-element.9.features_in, s32[64,256]{1,0:T(8,128)} %bitcast.11, s32[16]{0:T(128)} %bitcast.12, s32[32]{0:T(128)} %bitcast.13), custom_call_target="tpu_custom_call" | custom-call | tf_op jit(solution)/shard_map/pallas_call | solution.py:484
  58.1 16.2 %shard_map.84 = f32[64,144]{1,0:T(8,128)} custom-call(f32[32,40,128]{2,1,0:T(8,128)} %get-tuple-element.11.upper, f32[32,40,128]{2,1,0:T(8,128)} %get-tuple-element.12.lower), custom_call_target="tpu_custom_call" | custom-call | tf_op jit(solution)/shard_map/pallas_call | solution.py:637
  74.3 1.5 %copy.10 = f32[1,1,144,64]{2,3,1,0:T(8,128)} copy(f32[1,1,144,64]{2,3,1,0:T(8,128)} %bitcast.9) | data formatting | bytes 73728

commit v9 on v8

--- a/solution.py
+++ b/solution.py
@@ -33,6 +33,7 @@
 SENT = EB + EB // 4
 PIECE = SENT // 2
 GROUP = 8
+CHUNK = 4
 FAR = -1e30
 STEP = ZY + 1
 AHEAD = 4
@@ -370,6 +371,7 @@
 
 def pool_kernel(
     features_in, index_in, touched_in, owner_in, upper, lower,
+    empty_upper, empty_lower, full_upper, full_lower, cleared, placed,
     features, index, touched, owner, row_a, row_b, merged, local, ahead, *rest,
 ):
     accs, targets = rest[:ACCS], rest[ACCS:]
@@ -409,6 +411,22 @@
     for k in range(AHEAD):
         fetch(k, k).start()
     lax.fori_loop(ROWS // 32, ROWS // 16, reset, 0)
+    lane = lax.broadcasted_iota(jnp.int32, (PIECE, HALF), 1)
+    row = lax.broadcasted_iota(jnp.int32, (PIECE, HALF), 0)
+    empty = jnp.where(lane >= 2 * FEATURES, 0.0, FAR)
+
+    def fill(b, carry):
+        empty_upper[b] = empty
+        empty_lower[b] = jnp.where(row < EB - PIECE, empty, 0.0)
+        return carry
+
+    lax.fori_loop(0, BLOCKS, fill, 0)
+    clearings = [
+        pltpu.make_async_copy(empty_upper, upper, cleared.at[0]),
+        pltpu.make_async_copy(empty_lower, lower, cleared.at[1]),
+    ]
+    for clearing in clearings:
+        clearing.start()
     ones = jnp.ones((1, HALF), jnp.float32)
 
     def turn(n, row):
@@ -443,16 +461,8 @@
     loads[3].wait()
     loads[4].wait()
 
-    lane = lax.broadcasted_iota(jnp.int32, (EB, HALF), 1)
-    empty = jnp.where(lane >= 2 * FEATURES, 0.0, FAR)
-
-    def fill(b, carry):
-        upper[b] = empty[:PIECE]
-        lower[b, : EB - PIECE, :] = empty[PIECE:]
-        lower[b, EB - PIECE :, :] = jnp.zeros((SENT - EB, HALF), jnp.float32)
-        return carry
-
-    lax.fori_loop(0, BLOCKS, fill, 0)
+    for clearing in clearings:
+        clearing.wait()
     lane = lax.broadcasted_iota(jnp.int32, (EB // 4, HALF), 1)
 
     def place(i, carry):
@@ -466,17 +476,26 @@
         to = owner[touched[i]]
         tile_x, tile_yz = lax.rem(to, ROW), lax.div(to, ROW)
         extremes = merged[pl.ds(0, EB, stride=2), :]
-        upper[tile_x * GROUP + tile_yz] = extremes[:PIECE]
-        lower[to, : EB - PIECE, :] = extremes[PIECE:]
+        full_upper[i] = extremes[:PIECE]
+        full_lower[i, : EB - PIECE, :] = extremes[PIECE:]
         sums = merged[pl.ds(1, EB, stride=2), :]
         packed = jnp.zeros((EB // 4, HALF), jnp.float32)
         for j in range(4):
             group = pltpu.roll(sums[j * 16 : (j + 1) * 16], (32 * j - 16) % HALF, 1)
             packed = jnp.where((lane >= 32 * j) & (lane < 32 * j + 32), group, packed)
-        lower[to, EB - PIECE :, :] = packed
+        full_lower[i, EB - PIECE :, :] = packed
+        pltpu.make_async_copy(full_upper.at[i], upper.at[tile_x * GROUP + tile_yz], placed.at[0, i]).start()
+        pltpu.make_async_copy(full_lower.at[i], lower.at[to], placed.at[1, i]).start()
         return carry
 
     lax.fori_loop(0, TOUCH, place, 0)
+
+    def settle(i, carry):
+        pltpu.make_async_copy(full_upper.at[i], upper.at[0], placed.at[0, i]).wait()
+        pltpu.make_async_copy(full_lower.at[i], lower.at[0], placed.at[1, i]).wait()
+        return carry
+
+    lax.fori_loop(0, TOUCH, settle, 0)
 
 
 def pooled(features, index, touched, owner):
@@ -485,8 +504,11 @@
         pool_kernel,
         out_shape=[jax.ShapeDtypeStruct((BLOCKS, PIECE, HALF), jnp.float32)] * 2,
         in_specs=[hbm] * 4,
-        out_specs=[pl.BlockSpec(memory_space=pltpu.VMEM)] * 2,
-        scratch_shapes=[
+        out_specs=[hbm] * 2,
+        scratch_shapes=[pltpu.VMEM((BLOCKS, PIECE, HALF), jnp.float32)] * 2
+        + [pltpu.VMEM((TOUCH, PIECE, HALF), jnp.float32)] * 2
+        + [pltpu.SemaphoreType.DMA((2,)), pltpu.SemaphoreType.DMA((2, TOUCH))]
+        + [
             pltpu.VMEM((2 * FEATURES * STEP, HALF), jnp.float32),
             pltpu.VMEM((ZY, X), jnp.int32),
             pltpu.SMEM((TOUCH,), jnp.int32),
@@ -550,21 +572,23 @@
             device_id_type=MESH,
         )
 
-    def first_upper(k):
-        source = upper.at[pl.ds(along_x(k) * GROUP, GROUP)]
-        return copy(source, upper_got.at[k - 1], k - 1, yz * ROW + along_x(k))
-
-    def first_lower(k):
-        source = lower.at[pl.ds(along_y(k) * GROUP, GROUP)]
-        return copy(source, lower_got.at[k - 1], ROW + k - 2, along_y(k) * GROUP + zx)
+    def first_upper(k, c):
+        source = upper.at[pl.ds(along_x(k) * GROUP + c * CHUNK, CHUNK)]
+        target = upper_got.at[k - 1, pl.ds(c * CHUNK, CHUNK)]
+        return copy(source, target, 2 * (k - 1) + c, yz * ROW + along_x(k))
+
+    def first_lower(k, c):
+        source = lower.at[pl.ds(along_y(k) * GROUP + c * CHUNK, CHUNK)]
+        target = lower_got.at[k - 1, pl.ds(c * CHUNK, CHUNK)]
+        return copy(source, target, 2 * (ROW + k - 2) + c, along_y(k) * GROUP + zx)
 
     def last_upper(k):
         source = upper_sum.at[along_yz(k)]
-        return copy(source, upper_last.at[k - 1], 2 * (ROW - 1) + k - 1, along_yz(k) * ROW + x)
+        return copy(source, upper_last.at[k - 1], 4 * (ROW - 1) + k - 1, along_yz(k) * ROW + x)
 
     def last_lower(k):
         source = lower_sum.at[along_zx(k)]
-        return copy(source, lower_last.at[k - 1], 2 * (ROW - 1) + GROUP + k - 2, y * GROUP + along_zx(k))
+        return copy(source, lower_last.at[k - 1], 4 * (ROW - 1) + GROUP + k - 2, y * GROUP + along_zx(k))
 
     lane = lax.broadcasted_iota(jnp.int32, (PIECE, HALF), 1)
     row = lax.broadcasted_iota(jnp.int32, (PIECE, HALF), 0)
@@ -575,29 +599,31 @@
         return jnp.where(adds, left + right, jnp.maximum(left, right))
 
     order = (2, 1, 3)
-    for k in order:
-        first_upper(k).start()
-        first_lower(k).start()
+    for c in range(2):
+        for k in order:
+            first_upper(k, c).start()
+            first_lower(k, c).start()
     for load in loads:
         load.wait()
 
-    def stage(adds, first, got, summed, last):
+    def stage(c, adds, first, got, summed, last, mine):
         for k in order:
-            first(k).wait_recv()
+            first(k, c).wait_recv()
 
         def one(b, carry):
             total = summed[b]
             for k in range(ROW - 1):
                 total = join(adds, total, got[k, b])
             summed[b] = total
+            away = lax.rem(b - mine + GROUP, GROUP)
+            pl.when(away != 0)(lambda: last(away).start())
             return carry
 
-        lax.fori_loop(0, GROUP, one, 0)
-        for k in range(1, GROUP):
-            last(k).start()
-
-    stage(upper_adds, first_upper, upper_got, upper_sum, last_upper)
-    stage(lower_adds, first_lower, lower_got, lower_sum, last_lower)
+        lax.fori_loop(c * CHUNK, (c + 1) * CHUNK, one, 0)
+
+    for c in range(2):
+        stage(c, upper_adds, first_upper, upper_got, upper_sum, last_upper, yz)
+        stage(c, lower_adds, first_lower, lower_got, lower_sum, last_lower, zx)
 
     def gather(adds, total, got, last):
         for k in range(1, GROUP):
@@ -624,8 +650,9 @@
     out[:, HALF:] = shifted[:, : 3 * FEATURES - HALF]
 
     for k in order:
-        first_upper(k).wait_send()
-        first_lower(k).wait_send()
+        for c in range(2):
+            first_upper(k, c).wait_send()
+            first_lower(k, c).wait_send()
     for k in range(1, GROUP):
         last_upper(k).wait_send()
         last_lower(k).wait_send()
@@ -633,7 +660,7 @@
 
 def merged_stats(upper, lower):
     hbm = pl.BlockSpec(memory_space=pltpu.HBM)
-    copies = 2 * (ROW - 1) + 2 * (GROUP - 1)
+    copies = 4 * (ROW - 1) + 2 * (GROUP - 1)
     return pl.pallas_call(
         merge_kernel,
         out_shape=jax.ShapeDtypeStruct((EB, 3 * FEATURES), jnp.float32),

time: 75.9 us -> 74.2 us (0.978)
  Pallas kernels: 74.3 us -> 72.5 us
    pallas_call x1, Pallas kernels: 16.2 us -> 14.6 us  [merged_stats(): pl.pallas_call(merge_kernel, out_shape=jax.ShapeDtypeStruct((EB, 3 * FEAT...]
where the time goes in v9:
time: 74.2 us; the launch traced here: 74 us
  Pallas kernels  72.5 us (98%)
  local copies, waits for them, and re-layouts  1.47 us (2%)
    pallas_call x1, Pallas kernels, filtered(): pl.pallas_call(filter_kernel, out_shape=(jax.ShapeDtypeStruct((2, FEATURE...  39.5 us
    pallas_call x1, Pallas kernels, pooled(): pl.pallas_call(pool_kernel, out_shape=[jax.ShapeDtypeStruct((BLOCKS, PIEC...  18.4 us
    pallas_call x1, Pallas kernels, merged_stats(): pl.pallas_call(merge_kernel, out_shape=jax.ShapeDtypeStruct((EB, 3 * FEAT...  14.6 us

profile of v9, /device:TPU:1, one launch (start us, length us, event | category | flops | bytes accessed | tf_op | source)
XLA Modules:
  0.0 74.0 jit_solution(3066531437583182652)
XLA Ops:
  0.0 39.5 %shard_map.82 = (f32[2,3120,128]{2,1,0:T(8,128)}, s32[2,32,256]{2,1,0:T(8,128)}) custom-call(f32[12,64,256]{2,1,0:T(8,128)} %bitcast.8, s32[64,256]{1,0:T(8,128)} %bitcast.10, bf16[2,512,384]{2,1,0:T(8,128)(2,1)} %constant.8.clone.near_in, bf16[2,512,192]{2,1,0:T(8,128)(2,1)} %constant.9.clone.far_in, bf16[256,768]{1,0:T(8,128)(2,1)} %constant.10.clone.along_hi_in, ...), custom_call_target="tpu_custom_call" | custom-call | tf_op jit(solution)/shard_map/pallas_call | solution.py:342
  39.5 18.4 %shard_map.83 = (f32[32,40,128]{2,1,0:T(8,128)}, f32[32,40,128]{2,1,0:T(8,128)}) custom-call(f32[2,3120,128]{2,1,0:T(8,128)} %get-tuple-element.9.features_in, s32[64,256]{1,0:T(8,128)} %bitcast.11, s32[16]{0:T(128)} %bitcast.12, s32[32]{0:T(128)} %bitcast.13), custom_call_target="tpu_custom_call" | custom-call | tf_op jit(solution)/shard_map/pallas_call | solution.py:503
  57.9 14.6 %shard_map.84 = f32[64,144]{1,0:T(8,128)} custom-call(f32[32,40,128]{2,1,0:T(8,128)} %get-tuple-element.11.upper, f32[32,40,128]{2,1,0:T(8,128)} %get-tuple-element.12.lower), custom_call_target="tpu_custom_call" | custom-call | tf_op jit(solution)/shard_map/pallas_call | solution.py:664
  72.5 1.5 %copy.10 = f32[1,1,144,64]{2,3,1,0:T(8,128)} copy(f32[1,1,144,64]{2,3,1,0:T(8,128)} %bitcast.9) | data formatting | bytes 73728

commit v10 on v9

--- a/solution.py
+++ b/solution.py
@@ -37,6 +37,7 @@
 FAR = -1e30
 STEP = ZY + 1
 AHEAD = 4
+TOGETHER = 4
 VMEM_BYTES = 62 * 2**20
 MESH = pl.DeviceIdType.MESH
 
@@ -375,6 +376,8 @@
     features, index, touched, owner, row_a, row_b, merged, local, ahead, *rest,
 ):
     accs, targets = rest[:ACCS], rest[ACCS:]
+    for k in range(AHEAD):
+        pltpu.make_async_copy(index_in.at[k], targets[k], ahead.at[k]).start()
     loads = [
         pltpu.make_async_copy(source, target, local.at[k])
         for k, (source, target) in enumerate(
@@ -406,11 +409,7 @@
     def fetch(k, row):
         return pltpu.make_async_copy(index.at[row], targets[k], ahead.at[k])
 
-    lax.fori_loop(0, ROWS // 32, reset, 0)
-    loads[0].wait()
-    for k in range(AHEAD):
-        fetch(k, k).start()
-    lax.fori_loop(ROWS // 32, ROWS // 16, reset, 0)
+    lax.fori_loop(0, ROWS // 16, reset, 0)
     lane = lax.broadcasted_iota(jnp.int32, (PIECE, HALF), 1)
     row = lax.broadcasted_iota(jnp.int32, (PIECE, HALF), 0)
     empty = jnp.where(lane >= 2 * FEATURES, 0.0, FAR)
@@ -442,6 +441,7 @@
             old = acc[at, :]
             acc[at, :] = jnp.where(pair, old + value, jnp.maximum(old, value))
 
+    loads[0].wait()
     loads[1].wait()
     turn(0, row_a)
 
@@ -465,30 +465,35 @@
         clearing.wait()
     lane = lax.broadcasted_iota(jnp.int32, (EB // 4, HALF), 1)
 
-    def place(i, carry):
-        for k in range(2 * EB // 16):
-            rows = pl.ds(pl.multiple_of(i * 2 * EB + k * 16, 16), 16)
-            total = accs[0][rows, :]
-            for acc in accs[1:]:
-                more = acc[rows, :]
-                total = jnp.where(tile, total + more, jnp.maximum(total, more))
-            merged[pl.ds(k * 16, 16), :] = total
-        to = owner[touched[i]]
-        tile_x, tile_yz = lax.rem(to, ROW), lax.div(to, ROW)
-        extremes = merged[pl.ds(0, EB, stride=2), :]
-        full_upper[i] = extremes[:PIECE]
-        full_lower[i, : EB - PIECE, :] = extremes[PIECE:]
-        sums = merged[pl.ds(1, EB, stride=2), :]
-        packed = jnp.zeros((EB // 4, HALF), jnp.float32)
-        for j in range(4):
-            group = pltpu.roll(sums[j * 16 : (j + 1) * 16], (32 * j - 16) % HALF, 1)
-            packed = jnp.where((lane >= 32 * j) & (lane < 32 * j + 32), group, packed)
-        full_lower[i, EB - PIECE :, :] = packed
-        pltpu.make_async_copy(full_upper.at[i], upper.at[tile_x * GROUP + tile_yz], placed.at[0, i]).start()
-        pltpu.make_async_copy(full_lower.at[i], lower.at[to], placed.at[1, i]).start()
-        return carry
-
-    lax.fori_loop(0, TOUCH, place, 0)
+    def place(n, carry):
+        for u in range(TOGETHER):
+            for k in range(2 * EB // 16):
+                rows = pl.ds(pl.multiple_of((n * TOGETHER + u) * 2 * EB + k * 16, 16), 16)
+                total = accs[0][rows, :]
+                for acc in accs[1:]:
+                    more = acc[rows, :]
+                    total = jnp.where(tile, total + more, jnp.maximum(total, more))
+                merged[pl.ds(u * 2 * EB + k * 16, 16), :] = total
+        for u in range(TOGETHER):
+            i = n * TOGETHER + u
+            extremes = merged[pl.ds(u * 2 * EB, EB, stride=2), :]
+            full_upper[i] = extremes[:PIECE]
+            full_lower[i, : EB - PIECE, :] = extremes[PIECE:]
+            sums = merged[pl.ds(u * 2 * EB + 1, EB, stride=2), :]
+            packed = jnp.zeros((EB // 4, HALF), jnp.float32)
+            for j in range(4):
+                group = pltpu.roll(sums[j * 16 : (j + 1) * 16], (32 * j - 16) % HALF, 1)
+                packed = jnp.where((lane >= 32 * j) & (lane < 32 * j + 32), group, packed)
+            full_lower[i, EB - PIECE :, :] = packed
+        for u in range(TOGETHER):
+            i = n * TOGETHER + u
+            to = owner[touched[i]]
+            tile_x, tile_yz = lax.rem(to, ROW), lax.div(to, ROW)
+            pltpu.make_async_copy(full_upper.at[i], upper.at[tile_x * GROUP + tile_yz], placed.at[0, i]).start()
+            pltpu.make_async_copy(full_lower.at[i], lower.at[to], placed.at[1, i]).start()
+        return carry
+
+    lax.fori_loop(0, TOUCH // TOGETHER, place, 0)
 
     def settle(i, carry):
         pltpu.make_async_copy(full_upper.at[i], upper.at[0], placed.at[0, i]).wait()
@@ -514,7 +519,8 @@
             pltpu.SMEM((TOUCH,), jnp.int32),
             pltpu.SMEM((BLOCKS,), jnp.int32),
         ]
-        + [pltpu.VMEM((HALF, HALF), jnp.float32)] * 3
+        + [pltpu.VMEM((HALF, HALF), jnp.float32)] * 2
+        + [pltpu.VMEM((TOGETHER * HALF, HALF), jnp.float32)]
         + [pltpu.SemaphoreType.DMA((5,)), pltpu.SemaphoreType.DMA((AHEAD,))]
         + [pltpu.VMEM((ROWS, HALF), jnp.float32)] * ACCS
         + [pltpu.SMEM((X,), jnp.int32)] * AHEAD,

time: 74.2 us -> 73.2 us (0.987)
  Pallas kernels: 72.5 us -> 71.5 us
    pallas_call x1, Pallas kernels: 18.4 us -> 17.4 us  [pooled(): pl.pallas_call(pool_kernel, out_shape=[jax.ShapeDtypeStruct((BLOCKS, PIEC...]
where the time goes in v10:
time: 73.2 us; the launch traced here: 73 us
  Pallas kernels  71.5 us (98%)
  local copies, waits for them, and re-layouts  1.47 us (2%)
    pallas_call x1, Pallas kernels, filtered(): pl.pallas_call(filter_kernel, out_shape=(jax.ShapeDtypeStruct((2, FEATURE...  39.5 us
    pallas_call x1, Pallas kernels, pooled(): pl.pallas_call(pool_kernel, out_shape=[jax.ShapeDtypeStruct((BLOCKS, PIEC...  17.4 us
    pallas_call x1, Pallas kernels, merged_stats(): pl.pallas_call(merge_kernel, out_shape=jax.ShapeDtypeStruct((EB, 3 * FEAT...  14.6 us
    unnamed x1, local copies, waits for them, and re-layouts  1.47 us

profile of v10, /device:TPU:1, one launch (start us, length us, event | category | flops | bytes accessed | tf_op | source)
XLA Modules:
  0.0 73.0 jit_solution(12921801801750583389)
XLA Ops:
  0.0 39.5 %shard_map.82 = (f32[2,3120,128]{2,1,0:T(8,128)}, s32[2,32,256]{2,1,0:T(8,128)}) custom-call(f32[12,64,256]{2,1,0:T(8,128)} %bitcast.8, s32[64,256]{1,0:T(8,128)} %bitcast.10, bf16[2,512,384]{2,1,0:T(8,128)(2,1)} %constant.8.clone.near_in, bf16[2,512,192]{2,1,0:T(8,128)(2,1)} %constant.9.clone.far_in, bf16[256,768]{1,0:T(8,128)(2,1)} %constant.10.clone.along_hi_in, ...), custom_call_target="tpu_custom_call" | custom-call | tf_op jit(solution)/shard_map/pallas_call | solution.py:343
  39.5 17.4 %shard_map.83 = (f32[32,40,128]{2,1,0:T(8,128)}, f32[32,40,128]{2,1,0:T(8,128)}) custom-call(f32[2,3120,128]{2,1,0:T(8,128)} %get-tuple-element.9.features_in, s32[64,256]{1,0:T(8,128)} %bitcast.11, s32[16]{0:T(128)} %bitcast.12, s32[32]{0:T(128)} %bitcast.13), custom_call_target="tpu_custom_call" | custom-call | tf_op jit(solution)/shard_map/pallas_call | solution.py:508
  56.9 14.6 %shard_map.84 = f32[64,144]{1,0:T(8,128)} custom-call(f32[32,40,128]{2,1,0:T(8,128)} %get-tuple-element.11.upper, f32[32,40,128]{2,1,0:T(8,128)} %get-tuple-element.12.lower), custom_call_target="tpu_custom_call" | custom-call | tf_op jit(solution)/shard_map/pallas_call | solution.py:670
  71.6 1.5 %copy.10 = f32[1,1,144,64]{2,3,1,0:T(8,128)} copy(f32[1,1,144,64]{2,3,1,0:T(8,128)} %bitcast.9) | data formatting | bytes 73728

commit v11 on v10

--- a/solution.py
+++ b/solution.py
@@ -39,6 +39,7 @@
 AHEAD = 4
 TOGETHER = 4
 VMEM_BYTES = 62 * 2**20
+MERGE_BYTES = 107 * 2**19
 MESH = pl.DeviceIdType.MESH
 
 
@@ -681,7 +682,7 @@
             pltpu.SemaphoreType.DMA((2,)),
         ],
         compiler_params=pltpu.CompilerParams(
-            collective_id=1, has_side_effects=True, vmem_limit_bytes=VMEM_BYTES
+            collective_id=1, has_side_effects=True, vmem_limit_bytes=MERGE_BYTES
         ),
     )(upper, lower)
 

time: 73.2 us -> 71.7 us (0.980)
  local copies, waits for them, and re-layouts: 1.47 us -> 0.63 us
    unnamed x1, local copies, waits for them, and re-layouts: 1.47 us -> 0.63 us
where the time goes in v11:
time: 71.7 us; the launch traced here: 71.6 us
  Pallas kernels  70.9 us (99%)
    pallas_call x1, Pallas kernels, filtered(): pl.pallas_call(filter_kernel, out_shape=(jax.ShapeDtypeStruct((2, FEATURE...  39.5 us
    pallas_call x1, Pallas kernels, pooled(): pl.pallas_call(pool_kernel, out_shape=[jax.ShapeDtypeStruct((BLOCKS, PIEC...  17.4 us
    pallas_call x1, Pallas kernels, merged_stats(): pl.pallas_call(merge_kernel, out_shape=jax.ShapeDtypeStruct((EB, 3 * FEAT...  14.1 us

profile of v11, /device:TPU:1, one launch (start us, length us, event | category | flops | bytes accessed | tf_op | source)
XLA Modules:
  0.0 71.6 jit_solution(15951896524326767769)
XLA Ops:
  0.0 39.5 %shard_map.82 = (f32[2,3120,128]{2,1,0:T(8,128)}, s32[2,32,256]{2,1,0:T(8,128)}) custom-call(f32[12,64,256]{2,1,0:T(8,128)} %bitcast.9, s32[64,256]{1,0:T(8,128)} %bitcast.10, bf16[2,512,384]{2,1,0:T(8,128)(2,1)} %constant.8.clone.near_in, bf16[2,512,192]{2,1,0:T(8,128)(2,1)} %constant.9.clone.far_in, bf16[256,768]{1,0:T(8,128)(2,1)} %constant.10.clone.along_hi_in, ...), custom_call_target="tpu_custom_call" | custom-call | tf_op jit(solution)/shard_map/pallas_call | solution.py:344
  39.5 17.4 %shard_map.83 = (f32[32,40,128]{2,1,0:T(8,128)}, f32[32,40,128]{2,1,0:T(8,128)}) custom-call(f32[2,3120,128]{2,1,0:T(8,128)} %get-tuple-element.9.features_in, s32[64,256]{1,0:T(8,128)} %bitcast.11, s32[16]{0:T(128)} %bitcast.12, s32[32]{0:T(128)} %bitcast.13), custom_call_target="tpu_custom_call" | custom-call | tf_op jit(solution)/shard_map/pallas_call | solution.py:509
  56.9 14.1 %shard_map.84 = f32[64,144]{1,0:T(8,128)S(1)} custom-call(f32[32,40,128]{2,1,0:T(8,128)} %get-tuple-element.11.upper, f32[32,40,128]{2,1,0:T(8,128)} %get-tuple-element.12.lower), custom_call_target="tpu_custom_call" | custom-call | tf_op jit(solution)/shard_map/pallas_call | solution.py:671
  71.0 0.6 copy.10

commit v12 on v11

--- a/solution.py
+++ b/solution.py
@@ -112,8 +112,8 @@
         for k, (source, target) in enumerate(
             (
                 (raw, win.at[slot(0, 0)]),
-                (faces_in.at[:, pl.ds(0, HALF)], faces.at[0]),
-                (faces_in.at[:, pl.ds(HALF, HALF)], faces.at[1]),
+                (faces_in.at[:, pl.ds(0, HALF)], faces.at[0, pl.ds(0, ZY)]),
+                (faces_in.at[:, pl.ds(HALF, HALF)], faces.at[1, pl.ds(0, ZY)]),
                 (near_in.at[odd], near),
                 (far_in.at[odd], far),
                 (along_hi_in, along_hi),
@@ -351,7 +351,7 @@
         out_specs=(hbm, pl.BlockSpec(memory_space=pltpu.VMEM)),
         scratch_shapes=[
             pltpu.VMEM((9, C, ZY, X), jnp.float32),
-            pltpu.VMEM((2, ZY, HALF), jnp.int32),
+            pltpu.VMEM((2, ZY + 8, HALF), jnp.int32),
             pltpu.VMEM((C, 4 * ZY, X), jnp.float32),
             pltpu.VMEM((2, FEATURES * STEP, HALF), jnp.float32),
             pltpu.VMEM(near.shape[1:], jnp.bfloat16),
@@ -515,13 +515,13 @@
         + [pltpu.VMEM((TOUCH, PIECE, HALF), jnp.float32)] * 2
         + [pltpu.SemaphoreType.DMA((2,)), pltpu.SemaphoreType.DMA((2, TOUCH))]
         + [
-            pltpu.VMEM((2 * FEATURES * STEP, HALF), jnp.float32),
+            pltpu.VMEM((2 * FEATURES * STEP + ZY + 8, HALF), jnp.float32),
             pltpu.VMEM((ZY, X), jnp.int32),
             pltpu.SMEM((TOUCH,), jnp.int32),
             pltpu.SMEM((BLOCKS,), jnp.int32),
         ]
         + [pltpu.VMEM((HALF, HALF), jnp.float32)] * 2
-        + [pltpu.VMEM((TOGETHER * HALF, HALF), jnp.float32)]
+        + [pltpu.VMEM((TOGETHER * HALF + 8, HALF), jnp.float32)]
         + [pltpu.SemaphoreType.DMA((5,)), pltpu.SemaphoreType.DMA((AHEAD,))]
         + [pltpu.VMEM((ROWS, HALF), jnp.float32)] * ACCS
         + [pltpu.SMEM((X,), jnp.int32)] * AHEAD,

time: 71.7 us -> 71.8 us (level)
  no operation moved by 1% of the time
where the time goes in v12:
time: 71.8 us; the launch traced here: 71.7 us
  Pallas kernels  71 us (99%)
    pallas_call x1, Pallas kernels, filtered(): pl.pallas_call(filter_kernel, out_shape=(jax.ShapeDtypeStruct((2, FEATURE...  39.5 us
    pallas_call x1, Pallas kernels, pooled(): pl.pallas_call(pool_kernel, out_shape=[jax.ShapeDtypeStruct((BLOCKS, PIEC...  17.5 us
    pallas_call x1, Pallas kernels, merged_stats(): pl.pallas_call(merge_kernel, out_shape=jax.ShapeDtypeStruct((EB, 3 * FEAT...  14 us

profile of v12, /device:TPU:1, one launch (start us, length us, event | category | flops | bytes accessed | tf_op | source)
XLA Modules:
  0.0 71.7 jit_solution(16726032007901527723)
XLA Ops:
  0.0 39.5 %shard_map.82 = (f32[2,3120,128]{2,1,0:T(8,128)}, s32[2,32,256]{2,1,0:T(8,128)}) custom-call(f32[12,64,256]{2,1,0:T(8,128)} %bitcast.9, s32[64,256]{1,0:T(8,128)} %bitcast.10, bf16[2,512,384]{2,1,0:T(8,128)(2,1)} %constant.8.clone.near_in, bf16[2,512,192]{2,1,0:T(8,128)(2,1)} %constant.9.clone.far_in, bf16[256,768]{1,0:T(8,128)(2,1)} %constant.10.clone.along_hi_in, ...), custom_call_target="tpu_custom_call" | custom-call | tf_op jit(solution)/shard_map/pallas_call | solution.py:344
  39.5 17.5 %shard_map.83 = (f32[32,40,128]{2,1,0:T(8,128)}, f32[32,40,128]{2,1,0:T(8,128)}) custom-call(f32[2,3120,128]{2,1,0:T(8,128)} %get-tuple-element.9.features_in, s32[64,256]{1,0:T(8,128)} %bitcast.11, s32[16]{0:T(128)} %bitcast.12, s32[32]{0:T(128)} %bitcast.13), custom_call_target="tpu_custom_call" | custom-call | tf_op jit(solution)/shard_map/pallas_call | solution.py:509
  57.0 14.0 %shard_map.84 = f32[64,144]{1,0:T(8,128)S(1)} custom-call(f32[32,40,128]{2,1,0:T(8,128)} %get-tuple-element.11.upper, f32[32,40,128]{2,1,0:T(8,128)} %get-tuple-element.12.lower), custom_call_target="tpu_custom_call" | custom-call | tf_op jit(solution)/shard_map/pallas_call | solution.py:671
  71.0 0.6 copy.10
